TPU v7x, 256 devices: a whole 4x4x8 slice. The times are simulated.
256 devices in a mesh: region: 64 (over z, y, x_hi), orb: 4 (over x_lo, core).
Axes of the slice: x: 4 (x_hi: 2, x_lo: 2; x = x_hi * 2 + x_lo), y: 4, z: 8, core: 2. Of those that a mesh axis runs over, the one named last changes fastest.
Arguments:
- orbitals: bfloat16 [2048, 49152], P(('orb', 'region')), may hold values from -1 to 1
- point_region: int32 [49152], replicated, may hold values from 0 to 63, as said below
- coulomb: bfloat16 [64, 4, 768, 768], P('region'), may hold values from 0.049804688 to 1
- pair_mask: int32 [64, 3], P('region'), may hold values 0 or 1
Outputs:
- exchange_out: float32 [2048, 49152], P('orb', 'region')
Inputs may be any that keep to these rules, and one draw needn't show every extreme that they name: `point_region`: each of the 64 regions holds exactly 768 points, and every aligned brick of 128 consecutive points lies in one region.
All inputs are finite; a program needn't handle non-finite values. No bound on the sum of `pair_mask` on one device may be relied on, other than what follows from the above.
Results may differ from a plain program's by a relative error of at most 0.0025.
Values may be sent and summed in bfloat16 or wider, within the bound.
No kernel may reach another device: no remote copies, remote signals or barrier semaphores. Data moves between devices by JAX's collectives and lax.ppermute only.
A program may use at most 128 MiB of HBM per device.

v0:
```python
import jax
import jax.numpy as jnp
from jax import lax
from jax.sharding import PartitionSpec as P

TILE = 128


def from_behind(shard, axis, by):
    size = lax.axis_size(axis)
    return lax.ppermute(shard, axis, [(i, (i + by) % size) for i in range(size)])


def cross(left, right):
    return lax.dot_general(
        left, right, (((0,), (0,)), ((), ())), preferred_element_type=jnp.float32
    )


def screened(partial_value, block, scale):
    gram = lax.psum(partial_value, "orb")
    return (gram * block.astype(jnp.float32)).astype(jnp.bfloat16) * scale


def per_device(orbitals, point_region, coulomb, pair_mask):
    count = orbitals.shape[0]
    npoints = orbitals.shape[1]
    bricks = npoints // TILE
    brick_region = point_region.reshape(bricks, TILE)[:, 0]
    order = jnp.argsort(brick_region, stable=True)
    grouped = jnp.take(orbitals.reshape(count, bricks, TILE), order, axis=1).reshape(count, npoints)
    own = lax.all_to_all(grouped, "region", split_axis=1, concat_axis=0, tiled=True)
    total = jnp.zeros(own.shape, jnp.float32)
    for offset in range(coulomb.shape[1]):
        if offset == 0:
            other = own
            scale = jnp.ones((), jnp.bfloat16)
        else:
            other = from_behind(own, "region", -offset)
            scale = pair_mask[0, offset - 1].astype(jnp.bfloat16)
        product = screened(cross(own, other), coulomb[0, offset], scale)
        total = total + lax.dot_general(
            other, product, (((1,), (1,)), ((), ())), preferred_element_type=jnp.float32
        )
        if offset > 0:
            reverse = jnp.dot(own, product, preferred_element_type=jnp.float32)
            total = total + from_behind(reverse.astype(jnp.bfloat16), "region", offset).astype(
                reverse.dtype
            )
    return -0.25 * total


def solution(mesh):
    in_specs = (P(("orb", "region"), None), P(), P("region", None, None, None), P("region", None))
    out_specs = P("orb", "region")
    return jax.shard_map(
        per_device, mesh=mesh, in_specs=in_specs, out_specs=out_specs, check_vma=False
    )
```

profile of v0, /device:TPU:126, one launch (start us, length us, event | category | flops | bytes accessed | tf_op | source)
XLA Modules:
  0.0 410.9 jit_solution(8811872158739789939)
XLA Ops:
  6.5 1.1 slice_reduce_fusion
  7.7 3.8 sort.17
  11.5 1.7 gather_fusion
  13.4 0.7 gather.7
  14.9 32.9 %all_to_all.16 = bf16[8,64,768]{2,0,1:T(8,128)(2,1)S(1)} all-to-all(bf16[8,64,768]{2,0,1:T(8,128)(2,1)S(1)} %copy.9), channel_id=1, replica_groups=mesh['region'=64,'orb'=4] {'region'}, dimensions={1} | all-to-all | bytes 1572864 | tf_op jit(solution)/shard_map/all_to_all | solution.py:32
  47.9 2.5 collective-permute-start
  50.4 0.5 collective-permute-start.2
  50.9 2.9 collective-permute-start.4
  53.8 2.2 convolution_bitcast_fusion
  56.1 41.5 %collective-permute-done = bf16[512,768]{1,0:T(8,128)(2,1)S(1)} collective-permute-done((bf16[512,768]{1,0:T(8,128)(2,1)S(1)}, bf16[512,768]{1,0:T(8,128)(2,1)S(1)}, u32[]{:S(2)}, u32[]{:S(2)}) %collective-permute-start) | collective-permute-done | bytes 786464 | tf_op jit(solution)/shard_map/ppermute | solution.py:11
  97.5 2.2 fusion.20
  99.7 5.5 %collective-permute-done.2 = bf16[512,768]{1,0:T(8,128)(2,1)S(1)} collective-permute-done((bf16[512,768]{1,0:T(8,128)(2,1)S(1)}, bf16[512,768]{1,0:T(8,128)(2,1)S(1)}, u32[]{:S(2)}, u32[]{:S(2)}) %collective-permute-start.2) | collective-permute-done | bytes 786464 | tf_op jit(solution)/shard_map/ppermute | solution.py:11
  105.2 2.3 fusion.17
  107.5 2.2 fusion.14
  109.8 0.6 copy-done.4
  110.4 0.7 fusion.23
  111.1 204.3 %all-reduce.3.cloned.1.call-done = (f32[768,768]{1,0:T(8,128)}, f32[768,768]{1,0:T(8,128)}, f32[768,768]{1,0:T(8,128)}, f32[768,768]{1,0:T(8,128)}) async-done(((f32[768,768]{1,0:T(8,128)}, f32[768,768]{1,0:T(8,128)}, f32[768,768]{1,0:T(8,128)}, f32[768,768]{1,0:T(8,128)}), (f32[768,768]{1,0:T(8,128)}, f32[768,768]{1,0:T(8,128)}, f32[768,768]{1,0:T(8,128)}, ...) | async-done | bytes 9437200 | tf_op jit(solution)/shard_map/psum | solution.py:21
  315.4 6.8 %fusion.6 = (bf16[768,768]{1,0:T(8,128)(2,1)S(1)}, bf16[768,768]{1,0:T(8,128)(2,1)S(1)}, bf16[768,768]{1,0:T(8,128)(2,1)S(1)}) fusion(f32[768,768]{1,0:T(8,128)} %get-tuple-element.9, bf16[1,4,768,768]{3,2,1,0:T(8,128)(2,1)} %param.6, bf16[]{:T(256)} %bitcast.10, bf16[]{:T(256)} %bitcast.14, f32[768,768]{1,0:T(8,128)} %get-tuple-element.7, bf16[]{:T(256)} %bitcast.12, ...), kind=kLoop, calls=%fused_computation.15 | loop fusion | flops 7077888 | bytes 14155782 | tf_op jit(solution)/shard_map/mul | solution.py:22
  322.2 0.8 convolution_convert_fusion.2
  323.0 3.4 collective-permute-start.1
  326.3 0.8 convolution_convert_fusion.1
  327.1 1.7 collective-permute-start.3
  328.9 0.8 convolution_convert_fusion
  329.7 3.4 collective-permute-start.5
  333.0 0.8 fusion.24
  333.9 0.8 fusion.25
  334.7 0.8 copy-done.1
  335.5 2.2 fusion.4
  337.7 27.0 %collective-permute-done.1 = bf16[512,768]{1,0:T(8,128)(2,1)S(1)} collective-permute-done((bf16[512,768]{1,0:T(8,128)(2,1)S(1)}, bf16[512,768]{1,0:T(8,128)(2,1)S(1)}, u32[]{:S(2)}, u32[]{:S(2)}) %collective-permute-start.1) | collective-permute-done | bytes 786464 | tf_op jit(solution)/shard_map/ppermute | solution.py:11
  364.7 21.0 %collective-permute-done.3 = bf16[512,768]{1,0:T(8,128)(2,1)S(1)} collective-permute-done((bf16[512,768]{1,0:T(8,128)(2,1)S(1)}, bf16[512,768]{1,0:T(8,128)(2,1)S(1)}, u32[]{:S(2)}, u32[]{:S(2)}) %collective-permute-start.3) | collective-permute-done | bytes 786464 | tf_op jit(solution)/shard_map/ppermute | solution.py:11
  385.6 16.2 %collective-permute-done.5 = bf16[512,768]{1,0:T(8,128)(2,1)S(1)} collective-permute-done((bf16[512,768]{1,0:T(8,128)(2,1)S(1)}, bf16[512,768]{1,0:T(8,128)(2,1)S(1)}, u32[]{:S(2)}, u32[]{:S(2)}) %collective-permute-start.5) | collective-permute-done | bytes 786464 | tf_op jit(solution)/shard_map/ppermute | solution.py:11
  401.8 2.2 add_multiply_fusion
  (22 shorter events, 1.0 us)
Async XLA Ops:
  6.5 5.0 %copy-start = (bf16[8,49152]{1,0:T(8,128)(2,1)S(1)}, bf16[8,49152]{1,0:T(8,128)(2,1)}, u32[]{:S(2)}) copy-start(bf16[8,49152]{1,0:T(8,128)(2,1)} %param.4) | copy-start | bytes 2359300
  6.5 308.8 %all-reduce.3.cloned.1.call-start = ((), (), s32[]{:S(2)}) async-start(), calls=%async_computation.1 | async-start | bytes 18874368 | tf_op jit(solution)/shard_map/psum | solution.py:21
  47.9 49.7 %collective-permute-start = (bf16[512,768]{1,0:T(8,128)(2,1)S(1)}, bf16[512,768]{1,0:T(8,128)(2,1)S(1)}, u32[]{:S(2)}, u32[]{:S(2)}) collective-permute-start(bf16[512,768]{1,0:T(8,128)(2,1)S(1)} %bitcast.60), channel_id=1, source_target_pairs={{0,252},{4,0},{8,4},{12,8},{16,12},{20,16},{24,20},{28,24},{32,28}... | collective-permute-start | bytes 2359304 | tf_op jit(solution)/shard_map/ppermute | solution.py:11
  50.4 54.8 %collective-permute-start.2 = (bf16[512,768]{1,0:T(8,128)(2,1)S(1)}, bf16[512,768]{1,0:T(8,128)(2,1)S(1)}, u32[]{:S(2)}, u32[]{:S(2)}) collective-permute-start(bf16[512,768]{1,0:T(8,128)(2,1)S(1)} %bitcast.61), channel_id=1, source_target_pairs={{0,248},{4,252},{8,0},{12,4},{16,8},{20,12},{24,16},{28,20},{32,24... | collective-permute-start | bytes 2359304 | tf_op jit(solution)/shard_map/ppermute | solution.py:11
  50.9 56.6 %collective-permute-start.4 = (bf16[512,768]{1,0:T(8,128)(2,1)S(1)}, bf16[512,768]{1,0:T(8,128)(2,1)S(1)}, u32[]{:S(2)}, u32[]{:S(2)}) collective-permute-start(bf16[512,768]{1,0:T(8,128)(2,1)S(1)} %bitcast.62), channel_id=1, source_target_pairs={{0,244},{4,248},{8,252},{12,0},{16,4},{20,8},{24,12},{28,16},{32,2... | collective-permute-start | bytes 2359304 | tf_op jit(solution)/shard_map/ppermute | solution.py:11
  105.2 2.3 copy-start.2
  109.7 0.7 copy-start.4
  323.0 41.7 %collective-permute-start.1 = (bf16[512,768]{1,0:T(8,128)(2,1)S(1)}, bf16[512,768]{1,0:T(8,128)(2,1)S(1)}, u32[]{:S(2)}, u32[]{:S(2)}) collective-permute-start(bf16[512,768]{1,0:T(8,128)(2,1)S(1)} %convolution_convert_fusion.2), channel_id=1, source_target_pairs={{0,4},{4,8},{8,12},{12,16},{16,20},{20,24},{24,28},{28,32},{32,36}... | collective-permute-start | bytes 2359304 | tf_op jit(solution)/shard_map/ppermute | solution.py:11
  327.1 58.5 %collective-permute-start.3 = (bf16[512,768]{1,0:T(8,128)(2,1)S(1)}, bf16[512,768]{1,0:T(8,128)(2,1)S(1)}, u32[]{:S(2)}, u32[]{:S(2)}) collective-permute-start(bf16[512,768]{1,0:T(8,128)(2,1)S(1)} %convolution_convert_fusion.1), channel_id=1, source_target_pairs={{0,8},{4,12},{8,16},{12,20},{16,24},{20,28},{24,32},{28,36},{32,40... | collective-permute-start | bytes 2359304 | tf_op jit(solution)/shard_map/ppermute | solution.py:11
  329.7 4.2 %copy-start.3 = (bf16[512,768]{1,0:T(8,128)(2,1)S(1)}, bf16[512,768]{1,0:T(8,128)(2,1)}, u32[]{:S(2)}) copy-start(bf16[512,768]{1,0:T(8,128)(2,1)} %copy-done.2) | copy-start | bytes 2359300
  329.7 72.1 %collective-permute-start.5 = (bf16[512,768]{1,0:T(8,128)(2,1)S(1)}, bf16[512,768]{1,0:T(8,128)(2,1)S(1)}, u32[]{:S(2)}, u32[]{:S(2)}) collective-permute-start(bf16[512,768]{1,0:T(8,128)(2,1)S(1)} %convolution_convert_fusion), channel_id=1, source_target_pairs={{0,12},{4,16},{8,20},{12,24},{16,28},{20,32},{24,36},{28,40},{32,4... | collective-permute-start | bytes 2359304 | tf_op jit(solution)/shard_map/ppermute | solution.py:11
  333.9 1.7 copy-start.1
Sparse Core Ops, SparseCore 0:
  109.9 205.4 all-reduce.2
where the time goes:
time: 415 us; the launch traced here: 411 us
  waiting for transfers between devices  315 us (76%)
  blocking collectives  32.9 us (8%)
  matrix products  17.3 us (4%)
  starting transfers between devices  14.5 us (3%)
  between operations  13.5 us (3%)
  other arithmetic  10.7 us (3%)
  local copies, waits for them, and re-layouts  6.58 us (2%)
    psum x1, waiting for transfers between devices, screened(): gram = lax.psum(partial_value, 'orb')  204 us
    ppermute x6, waiting for transfers between devices, from_behind(): lax.ppermute(shard, axis, [(i, (i + by) % size) for i in range(size)])  111 us
    all_to_all x1, blocking collectives, per_device(): lax.all_to_all(grouped, 'region', split_axis=1, concat_axis=0, tiled=True)  32.9 us
    ppermute x6, starting transfers between devices, from_behind(): lax.ppermute(shard, axis, [(i, (i + by) % size) for i in range(size)])  14.5 us
    dot_general x4, matrix products, cross(): lax.dot_general(left, right, (((0,), (0,)), ((), ())), preferred_element_...  8.95 us
  transfers between devices with their start and end apart: 7, of which 6 were waited for; matrix products, arithmetic and copies ran while one was open for 3% of the time, Pallas kernels for 0%

commit v1 on v0

v1 whole, which is shorter than its diff:
```python
import jax
import jax.numpy as jnp
from jax import lax
from jax.sharding import PartitionSpec as P

TILE = 128


def moved(array, regions, chips=0, cores=0):
    size, orbs = lax.axis_size("region"), lax.axis_size("orb")
    pairs = [
        (r * orbs + o, (r + regions) % size * orbs + (o ^ (2 * chips + cores)))
        for r in range(size)
        for o in range(orbs)
    ]
    return lax.ppermute(array, ("region", "orb"), pairs)


def cross(left, right):
    return lax.dot_general(
        left, right, (((0,), (0,)), ((), ())), preferred_element_type=jnp.float32
    )


def onto_rows(orbs, product):
    return lax.dot_general(
        orbs, product, (((1,), (1,)), ((), ())), preferred_element_type=jnp.float32
    )


def onto_columns(orbs, product):
    return jnp.dot(orbs, product, preferred_element_type=jnp.float32)


def per_device(orbitals, point_region, coulomb, pair_mask):
    count = orbitals.shape[0]
    npoints = orbitals.shape[1]
    bricks = npoints // TILE
    core = lax.axis_index("orb") % 2
    half = coulomb.shape[2] // 2
    weights = pair_mask[0].astype(jnp.bfloat16)

    rows = lax.dynamic_slice_in_dim(coulomb[0], core * half, half, axis=1)
    away = jnp.stack([rows[1] * weights[0], rows[3] * weights[2]])
    behind = moved(away, 1, chips=1)

    brick_region = point_region.reshape(bricks, TILE)[:, 0]
    order = jnp.argsort(brick_region, stable=True)
    grouped = jnp.take(orbitals.reshape(count, bricks, TILE), order, axis=1).reshape(count, npoints)
    own = lax.all_to_all(grouped, "region", split_axis=1, concat_axis=0, tiled=True)
    prev = moved(own, 1)
    ahead = moved(own, -2)

    def on_chip(block):
        return jnp.concatenate([block, moved(block, 0, cores=1)], axis=0)

    def screened(left, right, block):
        mine = lax.dynamic_slice_in_dim(left, core * half, half, axis=1)
        partial = cross(mine, right)
        gram = partial + moved(partial.astype(jnp.bfloat16), 0, chips=1).astype(jnp.float32)
        product = (gram * block.astype(jnp.float32)).astype(jnp.bfloat16)
        other = moved(product, 0, cores=1)
        first = core == 0
        return jnp.concatenate(
            [jnp.where(first, product, other), jnp.where(first, other, product)], axis=0
        )

    own_chip, prev_chip, ahead_chip = on_chip(own), on_chip(prev), on_chip(ahead)
    self_pair = screened(own_chip, own_chip, rows[0])
    prev_own = screened(prev_chip, own_chip, behind[0])
    prev_ahead = screened(prev_chip, ahead_chip, behind[1])
    own_ahead = screened(own_chip, ahead_chip, rows[2] * weights[1])

    to_prev = onto_rows(own, prev_own) + onto_rows(ahead, prev_ahead)
    to_ahead = onto_columns(own, own_ahead) + onto_columns(prev, prev_ahead)
    from_next = moved(to_prev.astype(jnp.bfloat16), -1)
    from_back = moved(to_ahead.astype(jnp.bfloat16), 2)
    total = onto_rows(own, self_pair) + onto_rows(ahead, own_ahead) + onto_columns(prev, prev_own)
    total = total + from_next.astype(jnp.float32) + from_back.astype(jnp.float32)
    return -0.25 * total


def solution(mesh):
    in_specs = (P(("orb", "region"), None), P(), P("region", None, None, None), P("region", None))
    out_specs = P("orb", "region")
    return jax.shard_map(
        per_device, mesh=mesh, in_specs=in_specs, out_specs=out_specs, check_vma=False
    )
```

time: 415 us -> 173 us (0.42)
  waiting for transfers between devices: 315 us -> 76.4 us
  between operations: 13.5 us -> 0.25 us
  other arithmetic: 10.7 us -> 19 us
  starting transfers between devices: 14.5 us -> 21.2 us
    psum x1 -> x0, waiting for transfers between devices: 204 us -> none  [screened(): gram = lax.psum(partial_value, 'orb')]
    ppermute x6 -> x16, waiting for transfers between devices: 111 us -> 76.4 us  [moved(): return lax.ppermute(array, ('region', 'orb'), pairs)]
    convert_element_type x0 -> x3, other arithmetic: none -> 6.95 us  [the longest x2 6.94 us: screened(): product = (gram * block.astype(jnp.float32)).astype(jnp.bfloat16)]
    ppermute x6 -> x16, starting transfers between devices: 14.5 us -> 21.2 us  [moved(): return lax.ppermute(array, ('region', 'orb'), pairs)]
  transfers between devices with their start and end apart: 7 -> 16, of which waited for: 6 -> 9; matrix products, arithmetic and copies ran while one was open for 3% -> 18% of each run, Pallas kernels for 0% -> 0%
where the time goes in v1:
time: 173 us
  waiting for transfers between devices  76.4 us (44%)
  blocking collectives  32.9 us (19%)
  starting transfers between devices  21.2 us (12%)
  other arithmetic  19 us (11%)
  matrix products  16 us (9%)
  local copies, waits for them, and re-layouts  7.05 us (4%)
    ppermute x16, waiting for transfers between devices, moved(): return lax.ppermute(array, ('region', 'orb'), pairs)  76.4 us
    all_to_all x1, blocking collectives, per_device(): lax.all_to_all(grouped, 'region', split_axis=1, concat_axis=0, tiled=True)  32.9 us
    ppermute x16, starting transfers between devices, moved(): return lax.ppermute(array, ('region', 'orb'), pairs)  21.2 us
    dot_general x4, matrix products, cross(): lax.dot_general(left, right, (((0,), (0,)), ((), ())), preferred_element_...  10.4 us
    convert_element_type x2, other arithmetic, screened(): product = (gram * block.astype(jnp.float32)).astype(jnp.bfloat16)  6.94 us
    sort x1, other arithmetic, per_device(): order = jnp.argsort(brick_region, stable=True)  3.77 us
  transfers between devices with their start and end apart: 16, of which 9 were waited for; matrix products, arithmetic and copies ran while one was open for 18% of the time, Pallas kernels for 0%

profile of v1, /device:TPU:126, one launch (start us, length us, event | category | flops | bytes accessed | tf_op | source)
XLA Modules:
  0.0 172.9 jit_solution(14546209969560980367)
XLA Ops:
  0.0 1.1 slice_reduce_fusion
  1.2 3.8 %sort.17 = (s32[384]{0:T(512)}, s32[384]{0:T(512)S(1)}) sort(s32[384]{0:T(512)S(1)} %slice_reduce_fusion, s32[384]{0:T(512)S(1)} %iota.4), dimensions={0}, to_apply=%region_0.1 | sort | flops 3456 | bytes 6144 | tf_op jit(solution)/shard_map/jit(argsort)/sort | solution.py:48
  5.3 1.7 %gather_fusion = bf16[384,8,128]{2,1,0:T(8,128)(2,1)S(1)} fusion(bf16[8,384,128]{2,0,1:T(8,128)(2,1)S(1)} %bitcast.49, s32[1024]{0:T(1024)S(1)} %pad_clamp_fusion), kind=kCustom, calls=%fused_computation | custom fusion | bytes 1574400 | tf_op jit(solution)/shard_map/jit(_take)/gather | solution.py:49
  8.4 32.9 %all_to_all.16 = bf16[8,64,768]{2,0,1:T(8,128)(2,1)S(1)} all-to-all(bf16[8,64,768]{2,0,1:T(8,128)(2,1)S(1)} %copy.9), channel_id=1, replica_groups=mesh['region'=64,'orb'=4] {'region'}, dimensions={1} | all-to-all | bytes 1572864 | tf_op jit(solution)/shard_map/all_to_all | solution.py:50
  41.5 7.2 %collective-permute-start.7 = (bf16[512,768]{1,0:T(8,128)(2,1)S(1)}, bf16[512,768]{1,0:T(8,128)(2,1)S(1)}, u32[]{:S(2)}, u32[]{:S(2)}) collective-permute-start(bf16[512,768]{1,0:T(8,128)(2,1)S(1)} %bitcast.51), channel_id=1, source_target_pairs={{0,4},{1,5},{2,6},{3,7},{4,8},{5,9},{6,10},{7,11},{8,12},{9,13},{1... | collective-permute-start | bytes 2359304 | tf_op jit(solution)/shard_map/ppermute | solution.py:16
  48.6 13.8 %collective-permute-done.3 = bf16[512,768]{1,0:T(8,128)(2,1)S(1)} collective-permute-done((bf16[512,768]{1,0:T(8,128)(2,1)S(1)}, bf16[512,768]{1,0:T(8,128)(2,1)S(1)}, u32[]{:S(2)}, u32[]{:S(2)}) %collective-permute-start.3) | collective-permute-done | bytes 786464 | tf_op jit(solution)/shard_map/ppermute | solution.py:16
  62.4 1.3 collective-permute-done.7
  64.9 2.8 %fusion.17 = (bf16[1,384,768]{2,1,0:T(8,128)(2,1)S(1)}, bf16[1,384,768]{2,1,0:T(8,128)(2,1)S(1)}) fusion(bf16[1,4,768,768]{3,2,1,0:T(8,128)(2,1)} %param.6, s32[]{:T(128)S(6)} %add.65, s32[]{:T(128)S(6)} %select_n.65, bf16[]{:T(256)} %bitcast.9, bf16[]{:T(256)} %bitcast.11, s32[]{:T(128)S(6)} %add.66), kind=kLoop, calls=%fused_computation.39 | loop fusion | flops 2359296 | bytes 2359312 | tf_op jit(solution)/shard_map/mul | solution.py:44
  67.7 1.1 pad_maximum_fusion.2
  68.8 8.2 %collective-permute-start.10 = (bf16[2,384,768]{2,1,0:T(8,128)(2,1)}, bf16[2,384,768]{2,1,0:T(8,128)(2,1)}, u32[]{:S(2)}, u32[]{:S(2)}) collective-permute-start(bf16[2,384,768]{2,1,0:T(8,128)(2,1)} %pad_maximum_fusion.2), channel_id=1, source_target_pairs={{0,6},{1,7},{2,4},{3,5},{4,10},{5,11},{6,8},{7,9},{8,14},{9,15},{1... | collective-permute-start | bytes 3538952 | tf_op jit(solution)/shard_map/ppermute | solution.py:16
  77.1 1.2 constant_dynamic-update-slice_fusion
  78.3 2.6 %fusion.39 = (bf16[384,768]{1,0:T(8,128)(2,1)}, f32[384,768]{1,0:T(8,128)S(1)}) fusion(bf16[1024,768]{1,0:T(8,128)(2,1)S(1)} %constant_dynamic-update-slice_fusion, s32[]{:T(128)S(6)} %select_n.65, bf16[512,768]{1,0:T(8,128)(2,1)S(1)} %collective-permute-done.7, bf16[512,768]{1,0:T(8,128)(2,1)} %collective-permute-done.8), kind=kOutput, calls=%fused_computation.74 | convolution fusion | flops 605847552 | bytes 4915204 | tf_op jit(solution)/shard_map/dot_general | solution.py:20
  80.9 3.0 %fusion.38 = (bf16[384,768]{1,0:T(8,128)(2,1)}, f32[384,768]{1,0:T(8,128)}) fusion(bf16[512,768]{1,0:T(8,128)(2,1)S(1)} %collective-permute-done, bf16[512,768]{1,0:T(8,128)(2,1)S(1)} %bitcast.53, s32[]{:T(128)S(6)} %select_n.65, bf16[512,768]{1,0:T(8,128)(2,1)S(1)} %collective-permute-done.7, bf16[512,768]{1,0:T(8,128)(2,1)} %collective-permute-done.8), kind=kOutput, calls=%fused_computation.73 | convolution fusion | flops 608993280 | bytes 4915204 | tf_op jit(solution)/shard_map/dot_general | solution.py:20
  83.9 2.0 %collective-permute-start.9 = (bf16[384,768]{1,0:T(8,128)(2,1)}, bf16[384,768]{1,0:T(8,128)(2,1)}, u32[]{:S(2)}, u32[]{:S(2)}) collective-permute-start(bf16[384,768]{1,0:T(8,128)(2,1)} %get-tuple-element.24), channel_id=1, source_target_pairs={{0,2},{1,3},{2,0},{3,1},{4,6},{5,7},{6,4},{7,5},{8,10},{9,11},{10,... | collective-permute-start | bytes 1769480 | tf_op jit(solution)/shard_map/ppermute | solution.py:16
  86.0 2.1 %fusion.40 = (bf16[384,768]{1,0:T(8,128)(2,1)}, f32[384,768]{1,0:T(8,128)}) fusion(bf16[512,768]{1,0:T(8,128)(2,1)S(1)} %collective-permute-done, bf16[512,768]{1,0:T(8,128)(2,1)S(1)} %bitcast.54, s32[]{:T(128)S(6)} %select_n.65), kind=kOutput, calls=%fused_computation.75 | convolution fusion | flops 608993280 | bytes 4915204 | tf_op jit(solution)/shard_map/dot_general | solution.py:20
  88.1 2.6 %fusion.41 = (bf16[384,768]{1,0:T(8,128)(2,1)}, f32[384,768]{1,0:T(8,128)S(1)}) fusion(bf16[1024,768]{1,0:T(8,128)(2,1)S(1)} %constant_dynamic-update-slice_fusion, s32[]{:T(128)S(6)} %select_n.65, bf16[512,768]{1,0:T(8,128)(2,1)} %bitcast.55, bf16[512,768]{1,0:T(8,128)(2,1)S(1)} %collective-permute-done), kind=kOutput, calls=%fused_computation.76 | convolution fusion | flops 605847552 | bytes 4915204 | tf_op jit(solution)/shard_map/dot_general | solution.py:20
  90.7 2.0 %collective-permute-start.5 = (bf16[384,768]{1,0:T(8,128)(2,1)}, bf16[384,768]{1,0:T(8,128)(2,1)}, u32[]{:S(2)}, u32[]{:S(2)}) collective-permute-start(bf16[384,768]{1,0:T(8,128)(2,1)} %get-tuple-element.30), channel_id=1, source_target_pairs={{0,2},{1,3},{2,0},{3,1},{4,6},{5,7},{6,4},{7,5},{8,10},{9,11},{10,... | collective-permute-start | bytes 1769480 | tf_op jit(solution)/shard_map/ppermute | solution.py:16
  92.7 10.1 %collective-permute-done.10 = bf16[2,384,768]{2,1,0:T(8,128)(2,1)} collective-permute-done((bf16[2,384,768]{2,1,0:T(8,128)(2,1)}, bf16[2,384,768]{2,1,0:T(8,128)(2,1)}, u32[]{:S(2)}, u32[]{:S(2)}) %collective-permute-start.10) | collective-permute-done | bytes 1179680 | tf_op jit(solution)/shard_map/ppermute | solution.py:16
  102.8 7.2 %collective-permute-done.9 = bf16[384,768]{1,0:T(8,128)(2,1)} collective-permute-done((bf16[384,768]{1,0:T(8,128)(2,1)}, bf16[384,768]{1,0:T(8,128)(2,1)}, u32[]{:S(2)}, u32[]{:S(2)}) %collective-permute-start.9) | collective-permute-done | bytes 589856 | tf_op jit(solution)/shard_map/ppermute | solution.py:16
  110.1 3.4 %fusion.5 = (bf16[384,768]{1,0:T(8,128)(2,1)}, bf16[384,768]{1,0:T(8,128)(2,1)}) fusion(f32[384,768]{1,0:T(8,128)} %get-tuple-element.25, bf16[384,768]{1,0:T(8,128)(2,1)} %collective-permute-done.9, bf16[2,384,768]{2,1,0:T(8,128)(2,1)} %collective-permute-done.10, f32[384,768]{1,0:T(8,128)S(1)} %get-tuple-element.27, ...), kind=kLoop, calls=%fused_computation.20 | loop fusion | flops 2949120 | bytes 5898240 | tf_op jit(solution)/shard_map/convert_element_type | solution.py:61
  113.5 9.2 %collective-permute-done.1 = bf16[384,768]{1,0:T(8,128)(2,1)} collective-permute-done((bf16[384,768]{1,0:T(8,128)(2,1)}, bf16[384,768]{1,0:T(8,128)(2,1)}, u32[]{:S(2)}, u32[]{:S(2)}) %collective-permute-start.1) | collective-permute-done | bytes 589856 | tf_op jit(solution)/shard_map/ppermute | solution.py:16
  122.7 11.5 %collective-permute-done.5 = bf16[384,768]{1,0:T(8,128)(2,1)} collective-permute-done((bf16[384,768]{1,0:T(8,128)(2,1)}, bf16[384,768]{1,0:T(8,128)(2,1)}, u32[]{:S(2)}, u32[]{:S(2)}) %collective-permute-start.5) | collective-permute-done | bytes 589856 | tf_op jit(solution)/shard_map/ppermute | solution.py:16
  134.2 3.5 %fusion.7 = (bf16[384,768]{1,0:T(8,128)(2,1)S(1)}, bf16[384,768]{1,0:T(8,128)(2,1)}) fusion(f32[384,768]{1,0:T(8,128)S(1)} %copy-done.4, bf16[384,768]{1,0:T(8,128)(2,1)} %collective-permute-done.1, bf16[1,4,768,768]{3,2,1,0:T(8,128)(2,1)} %param.6, s32[]{:T(128)S(6)} %select_n.65, bf16[]{:T(256)} %bitcast.7, s32[]{:T(128)S(6)} %add.64, ...), kind=kLoop, calls=%fused_computation.24 | loop fusion | flops 4128768 | bytes 5898250 | tf_op jit(solution)/shard_map/convert_element_type | solution.py:61
  138.3 1.3 broadcast_select_fusion.2
  139.6 1.1 collective-permute-done.6
  140.7 1.1 broadcast_select_fusion.6
  145.1 0.8 add_convert_fusion.1
  146.7 0.8 fusion.15
  148.4 0.8 fusion
  149.3 14.2 %collective-permute-done.15 = bf16[512,768]{1,0:T(8,128)(2,1)S(1)} collective-permute-done((bf16[512,768]{1,0:T(8,128)(2,1)S(1)}, bf16[512,768]{1,0:T(8,128)(2,1)S(1)}, u32[]{:S(2)}, u32[]{:S(2)}) %collective-permute-start.15) | collective-permute-done | bytes 786464 | tf_op jit(solution)/shard_map/ppermute | solution.py:16
  163.5 7.8 %collective-permute-done.14 = bf16[512,768]{1,0:T(8,128)(2,1)S(1)} collective-permute-done((bf16[512,768]{1,0:T(8,128)(2,1)S(1)}, bf16[512,768]{1,0:T(8,128)(2,1)S(1)}, u32[]{:S(2)}, u32[]{:S(2)}) %collective-permute-start.14) | collective-permute-done | bytes 786464 | tf_op jit(solution)/shard_map/ppermute | solution.py:16
  171.3 1.5 add_multiply_fusion
  (59 shorter events, 8.4 us)
Async XLA Ops:
  0.0 5.3 %copy-start = (bf16[8,49152]{1,0:T(8,128)(2,1)S(1)}, bf16[8,49152]{1,0:T(8,128)(2,1)}, u32[]{:S(2)}) copy-start(bf16[8,49152]{1,0:T(8,128)(2,1)} %param.4) | copy-start | bytes 2359300
  7.9 55.8 %copy-start.9 = (s32[1,3]{1,0:T(1,128)S(1)}, s32[1,3]{1,0:T(1,128)}, u32[]{:S(2)}) copy-start(s32[1,3]{1,0:T(1,128)} %param.7) | copy-start | bytes 40
  41.3 44.6 %copy-start.1 = (bf16[8,64,768]{2,0,1:T(8,128)(2,1)}, bf16[8,64,768]{2,0,1:T(8,128)(2,1)S(1)}, u32[]{:S(2)}) copy-start(bf16[8,64,768]{2,0,1:T(8,128)(2,1)S(1)} %all_to_all.16) | copy-start | bytes 2359300
  41.3 21.1 %collective-permute-start.3 = (bf16[512,768]{1,0:T(8,128)(2,1)S(1)}, bf16[512,768]{1,0:T(8,128)(2,1)S(1)}, u32[]{:S(2)}, u32[]{:S(2)}) collective-permute-start(bf16[512,768]{1,0:T(8,128)(2,1)S(1)} %bitcast.50), channel_id=1, source_target_pairs={{0,248},{1,249},{2,250},{3,251},{4,252},{5,253},{6,254},{7,255},{8... | collective-permute-start | bytes 2359304 | tf_op jit(solution)/shard_map/ppermute | solution.py:16
  41.5 22.3 %collective-permute-start.7 = (bf16[512,768]{1,0:T(8,128)(2,1)S(1)}, bf16[512,768]{1,0:T(8,128)(2,1)S(1)}, u32[]{:S(2)}, u32[]{:S(2)}) collective-permute-start(bf16[512,768]{1,0:T(8,128)(2,1)S(1)} %bitcast.51), channel_id=1, source_target_pairs={{0,4},{1,5},{2,6},{3,7},{4,8},{5,9},{6,10},{7,11},{8,12},{9,13},{1... | collective-permute-start | bytes 2359304 | tf_op jit(solution)/shard_map/ppermute | solution.py:16
  62.4 14.6 %copy-start.7 = (bf16[512,768]{1,0:T(8,128)(2,1)}, bf16[512,768]{1,0:T(8,128)(2,1)S(1)}, u32[]{:S(2)}) copy-start(bf16[512,768]{1,0:T(8,128)(2,1)S(1)} %collective-permute-done.3) | copy-start | bytes 2359300
  62.4 14.6 %collective-permute-start.4 = (bf16[512,768]{1,0:T(8,128)(2,1)S(1)}, bf16[512,768]{1,0:T(8,128)(2,1)}, u32[]{:S(2)}, u32[]{:S(2)}) collective-permute-start(bf16[512,768]{1,0:T(8,128)(2,1)S(1)} %collective-permute-done.3), channel_id=1, source_target_pairs={{0,1},{1,0},{2,3},{3,2},{4,5},{5,4},{6,7},{7,6},{8,9},{9,8},{10,11... | collective-permute-start | bytes 2359304 | tf_op jit(solution)/shard_map/ppermute | solution.py:16
  63.7 17.2 %copy-start.5 = (bf16[512,768]{1,0:T(8,128)(2,1)}, bf16[512,768]{1,0:T(8,128)(2,1)S(1)}, u32[]{:S(2)}) copy-start(bf16[512,768]{1,0:T(8,128)(2,1)S(1)} %collective-permute-done.7) | copy-start | bytes 2359300
  63.7 14.5 %collective-permute-start.8 = (bf16[512,768]{1,0:T(8,128)(2,1)S(1)}, bf16[512,768]{1,0:T(8,128)(2,1)}, u32[]{:S(2)}, u32[]{:S(2)}) collective-permute-start(bf16[512,768]{1,0:T(8,128)(2,1)S(1)} %collective-permute-done.7), channel_id=1, source_target_pairs={{0,1},{1,0},{2,3},{3,2},{4,5},{5,4},{6,7},{7,6},{8,9},{9,8},{10,11... | collective-permute-start | bytes 2359304 | tf_op jit(solution)/shard_map/ppermute | solution.py:16
  64.5 16.4 %collective-permute-start = (bf16[512,768]{1,0:T(8,128)(2,1)S(1)}, bf16[512,768]{1,0:T(8,128)(2,1)S(1)}, u32[]{:S(2)}, u32[]{:S(2)}) collective-permute-start(bf16[512,768]{1,0:T(8,128)(2,1)S(1)} %bitcast.52), channel_id=1, source_target_pairs={{0,1},{1,0},{2,3},{3,2},{4,5},{5,4},{6,7},{7,6},{8,9},{9,8},{10,11... | collective-permute-start | bytes 2359304 | tf_op jit(solution)/shard_map/ppermute | solution.py:16
  68.8 34.0 %collective-permute-start.10 = (bf16[2,384,768]{2,1,0:T(8,128)(2,1)}, bf16[2,384,768]{2,1,0:T(8,128)(2,1)}, u32[]{:S(2)}, u32[]{:S(2)}) collective-permute-start(bf16[2,384,768]{2,1,0:T(8,128)(2,1)} %pad_maximum_fusion.2), channel_id=1, source_target_pairs={{0,6},{1,7},{2,4},{3,5},{4,10},{5,11},{6,8},{7,9},{8,14},{9,15},{1... | collective-permute-start | bytes 3538952 | tf_op jit(solution)/shard_map/ppermute | solution.py:16
  80.9 21.9 %collective-permute-start.12 = (bf16[384,768]{1,0:T(8,128)(2,1)}, bf16[384,768]{1,0:T(8,128)(2,1)}, u32[]{:S(2)}, u32[]{:S(2)}) collective-permute-start(bf16[384,768]{1,0:T(8,128)(2,1)} %get-tuple-element.26), channel_id=1, source_target_pairs={{0,2},{1,3},{2,0},{3,1},{4,6},{5,7},{6,4},{7,5},{8,10},{9,11},{10,... | collective-permute-start | bytes 1769480 | tf_op jit(solution)/shard_map/ppermute | solution.py:16
  83.9 26.1 %collective-permute-start.9 = (bf16[384,768]{1,0:T(8,128)(2,1)}, bf16[384,768]{1,0:T(8,128)(2,1)}, u32[]{:S(2)}, u32[]{:S(2)}) collective-permute-start(bf16[384,768]{1,0:T(8,128)(2,1)} %get-tuple-element.24), channel_id=1, source_target_pairs={{0,2},{1,3},{2,0},{3,1},{4,6},{5,7},{6,4},{7,5},{8,10},{9,11},{10,... | collective-permute-start | bytes 1769480 | tf_op jit(solution)/shard_map/ppermute | solution.py:16
  88.0 34.7 %collective-permute-start.1 = (bf16[384,768]{1,0:T(8,128)(2,1)}, bf16[384,768]{1,0:T(8,128)(2,1)}, u32[]{:S(2)}, u32[]{:S(2)}) collective-permute-start(bf16[384,768]{1,0:T(8,128)(2,1)} %get-tuple-element.28), channel_id=1, source_target_pairs={{0,2},{1,3},{2,0},{3,1},{4,6},{5,7},{6,4},{7,5},{8,10},{9,11},{10,... | collective-permute-start | bytes 1769480 | tf_op jit(solution)/shard_map/ppermute | solution.py:16
  90.7 43.5 %collective-permute-start.5 = (bf16[384,768]{1,0:T(8,128)(2,1)}, bf16[384,768]{1,0:T(8,128)(2,1)}, u32[]{:S(2)}, u32[]{:S(2)}) collective-permute-start(bf16[384,768]{1,0:T(8,128)(2,1)} %get-tuple-element.30), channel_id=1, source_target_pairs={{0,2},{1,3},{2,0},{3,1},{4,6},{5,7},{6,4},{7,5},{8,10},{9,11},{10,... | collective-permute-start | bytes 1769480 | tf_op jit(solution)/shard_map/ppermute | solution.py:16
  110.1 24.1 %copy-start.4 = (f32[384,768]{1,0:T(8,128)S(1)}, f32[384,768]{1,0:T(8,128)}, u32[]{:S(2)}) copy-start(f32[384,768]{1,0:T(8,128)} %get-tuple-element.29) | copy-start | bytes 3538948
  113.5 24.8 %collective-permute-start.13 = (bf16[384,768]{1,0:T(8,128)(2,1)}, bf16[384,768]{1,0:T(8,128)(2,1)}, u32[]{:S(2)}, u32[]{:S(2)}) collective-permute-start(bf16[384,768]{1,0:T(8,128)(2,1)} %get-tuple-element.16), channel_id=1, source_target_pairs={{0,1},{1,0},{2,3},{3,2},{4,5},{5,4},{6,7},{7,6},{8,9},{9,8},{10,11... | collective-permute-start | bytes 1769480 | tf_op jit(solution)/shard_map/ppermute | solution.py:16
  134.2 3.5 %copy-start.3 = (bf16[384,768]{1,0:T(8,128)(2,1)S(1)}, bf16[384,768]{1,0:T(8,128)(2,1)}, u32[]{:S(2)}) copy-start(bf16[384,768]{1,0:T(8,128)(2,1)} %get-tuple-element.15) | copy-start | bytes 1769476
  137.7 3.0 %collective-permute-start.6 = (bf16[384,768]{1,0:T(8,128)(2,1)}, bf16[384,768]{1,0:T(8,128)(2,1)S(1)}, u32[]{:S(2)}, u32[]{:S(2)}) collective-permute-start(bf16[384,768]{1,0:T(8,128)(2,1)} %get-tuple-element.8), channel_id=1, source_target_pairs={{0,1},{1,0},{2,3},{3,2},{4,5},{5,4},{6,7},{7,6},{8,9},{9,8},{10,11... | collective-permute-start | bytes 1769480 | tf_op jit(solution)/shard_map/ppermute | solution.py:16
  137.8 7.2 %collective-permute-start.11 = (bf16[384,768]{1,0:T(8,128)(2,1)S(1)}, bf16[384,768]{1,0:T(8,128)(2,1)S(1)}, u32[]{:S(2)}, u32[]{:S(2)}) collective-permute-start(bf16[384,768]{1,0:T(8,128)(2,1)S(1)} %copy-done.3), channel_id=1, source_target_pairs={{0,1},{1,0},{2,3},{3,2},{4,5},{5,4},{6,7},{7,6},{8,9},{9,8},{10,11... | collective-permute-start | bytes 1769480 | tf_op jit(solution)/shard_map/ppermute | solution.py:16
  138.3 10.0 %collective-permute-start.2 = (bf16[384,768]{1,0:T(8,128)(2,1)S(1)}, bf16[384,768]{1,0:T(8,128)(2,1)S(1)}, u32[]{:S(2)}, u32[]{:S(2)}) collective-permute-start(bf16[384,768]{1,0:T(8,128)(2,1)S(1)} %get-tuple-element.7), channel_id=1, source_target_pairs={{0,1},{1,0},{2,3},{3,2},{4,5},{5,4},{6,7},{7,6},{8,9},{9,8},{10,11... | collective-permute-start | bytes 1769480 | tf_op jit(solution)/shard_map/ppermute | solution.py:16
  139.6 2.3 %copy-start.6 = (bf16[512,768]{1,0:T(8,128)(2,1)S(1)}, bf16[512,768]{1,0:T(8,128)(2,1)}, u32[]{:S(2)}) copy-start(bf16[512,768]{1,0:T(8,128)(2,1)} %copy-done.5) | copy-start | bytes 2359300
  141.9 1.1 copy-start.2
  143.0 1.1 copy-start.8
  143.8 19.7 %collective-permute-start.15 = (bf16[512,768]{1,0:T(8,128)(2,1)S(1)}, bf16[512,768]{1,0:T(8,128)(2,1)S(1)}, u32[]{:S(2)}, u32[]{:S(2)}) collective-permute-start(bf16[512,768]{1,0:T(8,128)(2,1)S(1)} %add_convert_fusion), channel_id=1, source_target_pairs={{0,8},{1,9},{2,10},{3,11},{4,12},{5,13},{6,14},{7,15},{8,16},{9,17... | collective-permute-start | bytes 2359304 | tf_op jit(solution)/shard_map/ppermute | solution.py:16
  146.0 25.4 %collective-permute-start.14 = (bf16[512,768]{1,0:T(8,128)(2,1)S(1)}, bf16[512,768]{1,0:T(8,128)(2,1)S(1)}, u32[]{:S(2)}, u32[]{:S(2)}) collective-permute-start(bf16[512,768]{1,0:T(8,128)(2,1)S(1)} %add_convert_fusion.1), channel_id=1, source_target_pairs={{0,252},{1,253},{2,254},{3,255},{4,0},{5,1},{6,2},{7,3},{8,4},{9,5... | collective-permute-start | bytes 2359304 | tf_op jit(solution)/shard_map/ppermute | solution.py:16

commit v2 on v1

v2 whole, which is shorter than its diff:
```python
import functools

import jax
import jax.numpy as jnp
from jax import lax
from jax.experimental import pallas as pl
from jax.experimental.pallas import tpu as pltpu
from jax.sharding import PartitionSpec as P

TILE = 128


def moved(array, regions, chips=0, cores=0):
    size, orbs = lax.axis_size("region"), lax.axis_size("orb")
    pairs = [
        (r * orbs + o, (r + regions) % size * orbs + (o ^ (2 * chips + cores)))
        for r in range(size)
        for o in range(orbs)
    ]
    return lax.ppermute(array, ("region", "orb"), pairs)


def call(kernel, scalars, operands, in_specs, out_specs, out_shape, name):
    return pl.pallas_call(
        kernel,
        grid_spec=pltpu.PrefetchScalarGridSpec(
            num_scalar_prefetch=1, grid=(1,), in_specs=in_specs, out_specs=out_specs
        ),
        out_shape=out_shape,
        compiler_params=pltpu.CompilerParams(vmem_limit_bytes=24 * 2**20),
        cost_estimate=pl.CostEstimate(flops=0, bytes_accessed=0, transcendentals=0),
        name=name,
    )(scalars, *operands)


def whole(shape):
    return pl.BlockSpec(shape, lambda i, s: (0,) * len(shape))


def first_rows(left, right):
    return lax.dot_general(
        left, right, (((0,), (0,)), ((), ())), preferred_element_type=jnp.float32
    )


def onto_rows(orbs, product):
    return lax.dot_general(
        orbs, product, (((1,), (1,)), ((), ())), preferred_element_type=jnp.float32
    )


def onto_columns(orbs, product):
    return jnp.dot(orbs, product, preferred_element_type=jnp.float32)


def lanes(scalars, width):
    core = scalars[0]
    return (
        pl.ds(pl.multiple_of(core * width, TILE), width),
        pl.ds(pl.multiple_of((1 - core) * width, TILE), width),
    )


def gram_kernel(count, weight, scalars, *refs):
    lefts, rights, rest, out = refs[:count], refs[count : 2 * count], refs[2 * count : -1], refs[-1]
    total = sum(first_rows(left[...], right[...]) for left, right in zip(lefts, rights))
    if weight is None:
        out[...] = total
        return
    *partial, block = rest
    if partial:
        total = total + partial[0][...]
    total = (total * block[...].reshape(out.shape).astype(jnp.float32)).astype(jnp.bfloat16)
    if weight:
        total = total * scalars[weight].astype(jnp.bfloat16)
    out[...] = total


def gram(scalars, lefts, rights, partial=None, block=None, k=0):
    orbs, points = lefts[0].shape
    half = points // 2
    mine = pl.BlockSpec((orbs, half), lambda i, s: (0, s[0]))
    operands = [*lefts, *rights]
    specs = [mine] * len(lefts) + [whole((orbs, points))] * len(rights)
    if partial is not None:
        operands.append(partial)
        specs.append(whole((half, points)))
    if block is not None:
        operands.append(block)
        if block.ndim == 4:
            specs.append(pl.BlockSpec((1, 1, half, points), lambda i, s: (0, k, s[0], 0)))
        else:
            specs.append(pl.BlockSpec((half, points), lambda i, s: (k, 0)))
    weight = None if block is None else k if block.ndim == 4 else 0
    return call(
        functools.partial(gram_kernel, len(lefts), weight),
        scalars,
        operands,
        specs,
        whole((half, points)),
        jax.ShapeDtypeStruct((half, points), jnp.float32 if block is None else jnp.bfloat16),
        "gram",
    )


def away_kernel(scalars, one, three, out):
    half = out.shape[0] // 2
    out[:half] = one[0, 0] * scalars[1].astype(out.dtype)
    out[half:] = three[0, 0] * scalars[3].astype(out.dtype)


def away(scalars, coulomb):
    points = coulomb.shape[3]

    def block(k):
        return pl.BlockSpec((1, 1, points // 2, points), lambda i, s: (0, k, s[0], 0))

    return call(
        away_kernel,
        scalars,
        (coulomb, coulomb),
        [block(1), block(3)],
        whole((points, points)),
        jax.ShapeDtypeStruct((points, points), coulomb.dtype),
        "away",
    )


def to_prev_kernel(scalars, own, ahead, po, po_too, pa, pa_too, out):
    for part, by_own, by_ahead in zip(lanes(scalars, po.shape[0]), (po, po_too), (pa, pa_too)):
        total = onto_rows(own[...], by_own[...]) + onto_rows(ahead[...], by_ahead[...])
        out[:, part] = total.astype(out.dtype)


def to_ahead_kernel(scalars, own, prev, oa, oa_too, pa, pa_too, out):
    mine, other = lanes(scalars, oa.shape[0])
    total = onto_columns(own[:, mine], oa[...]) + onto_columns(own[:, other], oa_too[...])
    total += onto_columns(prev[:, mine], pa[...]) + onto_columns(prev[:, other], pa_too[...])
    out[...] = total.astype(out.dtype)


def stay_kernel(scalars, own, ahead, prev, oo, oo_too, oa, oa_too, po, po_too, out):
    mine, other = lanes(scalars, po.shape[0])
    out[...] = onto_columns(prev[:, mine], po[...]) + onto_columns(prev[:, other], po_too[...])
    for part, by_own, by_ahead in zip((mine, other), (oo, oo_too), (oa, oa_too)):
        out[:, part] += onto_rows(own[...], by_own[...]) + onto_rows(ahead[...], by_ahead[...])


def applied(kernel, scalars, orbs, products, dtype):
    shape = orbs[0].shape
    operands = (*orbs, *(p for pair in products for p in pair))
    return call(
        kernel,
        scalars,
        operands,
        [whole(o.shape) for o in operands],
        whole(shape),
        jax.ShapeDtypeStruct(shape, dtype),
        kernel.__name__,
    )


def per_device(orbitals, point_region, coulomb, pair_mask):
    count = orbitals.shape[0]
    npoints = orbitals.shape[1]
    bricks = npoints // TILE
    core = lax.axis_index("orb") % 2
    scalars = jnp.concatenate([core[None].astype(jnp.int32), pair_mask[0]])

    brick_region = point_region.reshape(bricks, TILE)[:, 0]
    order = jnp.argsort(brick_region, stable=True)
    grouped = jnp.take(orbitals.reshape(count, bricks, TILE), order, axis=1).reshape(count, npoints)
    own = lax.all_to_all(grouped, "region", split_axis=1, concat_axis=0, tiled=True)
    def beside(block):
        return moved(block, 0, cores=1)

    own_x = moved(own, 0, chips=1)
    prev_x = moved(own, 1, chips=1)
    ahead = moved(own, -2)
    own_s = beside(own)

    later, _ = lax.optimization_barrier((scalars, own))
    sent = away(later, coulomb)
    prev_x, own_x, ahead, sent = lax.optimization_barrier((prev_x, own_x, ahead, sent))
    behind = moved(sent, 1, chips=1)
    prev = moved(prev_x, 0, chips=1)
    ahead_x = moved(own_x, -2)
    own_xs, prev_xs, ahead_s = beside(own_x), beside(prev_x), beside(ahead)
    all_own = (own, own_s, own_x, own_xs)
    oo = gram(scalars, all_own, all_own, None, coulomb, 0)
    po = gram(scalars, (prev_x, prev_xs), (own_x, own_xs))
    oa = gram(scalars, (own, own_s), (ahead, ahead_s))
    ahead_x, prev, oo, po, oa = lax.optimization_barrier((ahead_x, prev, oo, po, oa))
    prev_s, ahead_xs = beside(prev), beside(ahead_x)
    oa = gram(scalars, (own_x, own_xs), (ahead_x, ahead_xs), oa, coulomb, 2)
    behind, oa = lax.optimization_barrier((behind, oa))
    po = gram(scalars, (prev, prev_s), (own, own_s), po, behind, 0)
    pa = gram(
        scalars,
        (prev, prev_s, prev_x, prev_xs),
        (ahead, ahead_s, ahead_x, ahead_xs),
        None,
        behind,
        1,
    )

    po, pa, oa, oo = ((p, beside(p)) for p in (po, pa, oa, oo))
    to_prev = applied(to_prev_kernel, scalars, (own_x, ahead_x), (po, pa), jnp.bfloat16)
    from_next = moved(to_prev, -1, chips=1)
    to_ahead = applied(to_ahead_kernel, scalars, (own, prev), (oa, pa), jnp.bfloat16)
    from_back = moved(to_ahead, 2)
    stay = applied(stay_kernel, scalars, (own, ahead, prev), (oo, oa, po), jnp.float32)
    return -0.25 * (stay + from_next.astype(jnp.float32) + from_back.astype(jnp.float32))


def solution(mesh):
    in_specs = (P(("orb", "region"), None), P(), P("region", None, None, None), P("region", None))
    out_specs = P("orb", "region")
    return jax.shard_map(
        per_device, mesh=mesh, in_specs=in_specs, out_specs=out_specs, check_vma=False
    )
```

time: 173 us -> 139 us (0.80)
  waiting for transfers between devices: 76.4 us -> 51.9 us
  Pallas kernels: 0 us -> 22.8 us
  matrix products: 16 us -> 0 us
  other arithmetic: 19 us -> 5.47 us
  starting transfers between devices: 21.2 us -> 17.6 us
    ppermute x16 -> x18, waiting for transfers between devices: 76.4 us -> 51.9 us  [moved(): return lax.ppermute(array, ('region', 'orb'), pairs)]
    pallas_call x0 -> x10, Pallas kernels: none -> 22.8 us  [call(): pl.pallas_call(kernel, grid_spec=pltpu.PrefetchScalarGridSpec(num_scalar_...]
    dot_general x11 -> x0, matrix products: 16 us -> none  [the longest x4 10.4 us: cross(): lax.dot_general(left, right, (((0,), (0,)), ((), ())), preferred_element_...]
    convert_element_type x3 -> x0, other arithmetic: 6.95 us -> none  [the longest x2 6.94 us: screened(): product = (gram * block.astype(jnp.float32)).astype(jnp.bfloat16)]
    unnamed x22 -> x11, local copies, waits for them, and re-layouts: 0.69 us -> 4.72 us
    ppermute x16 -> x18, starting transfers between devices: 21.2 us -> 17.6 us  [moved(): return lax.ppermute(array, ('region', 'orb'), pairs)]
    mul x2 -> x1, other arithmetic: 4.32 us -> 1.4 us  [per_device(): -0.25]
    select_n x4 -> x0, other arithmetic: 2.77 us -> none  [screened(): jnp.where(first, product, other)]
  transfers between devices with their start and end apart: 16 -> 18, of which waited for: 9 -> 11; matrix products, arithmetic and copies ran while one was open for 18% -> 0% of each run, Pallas kernels for 0% -> 16%
where the time goes in v2:
time: 139 us
  waiting for transfers between devices  51.9 us (37%)
  blocking collectives  32.9 us (24%)
  Pallas kernels  22.8 us (16%)
  starting transfers between devices  17.6 us (13%)
  local copies, waits for them, and re-layouts  7.89 us (6%)
  other arithmetic  5.47 us (4%)
    ppermute x18, waiting for transfers between devices, moved(): return lax.ppermute(array, ('region', 'orb'), pairs)  51.9 us
    all_to_all x1, blocking collectives, per_device(): lax.all_to_all(grouped, 'region', split_axis=1, concat_axis=0, tiled=True)  32.9 us
    pallas_call x10, Pallas kernels, call(): pl.pallas_call(kernel, grid_spec=pltpu.PrefetchScalarGridSpec(num_scalar_...  22.8 us
    ppermute x18, starting transfers between devices, moved(): return lax.ppermute(array, ('region', 'orb'), pairs)  17.6 us
    unnamed x11, local copies, waits for them, and re-layouts  4.72 us
    sort x1, other arithmetic, per_device(): order = jnp.argsort(brick_region, stable=True)  3.77 us
  transfers between devices with their start and end apart: 18, of which 11 were waited for; matrix products, arithmetic and copies ran while one was open for 0% of the time, Pallas kernels for 16%

profile of v2, /device:TPU:126, one launch (start us, length us, event | category | flops | bytes accessed | tf_op | source)
XLA Modules:
  0.0 138.8 jit_solution(2817649979767045629)
XLA Ops:
  0.0 1.1 slice_reduce_fusion
  1.2 3.8 %sort.17 = (s32[384]{0:T(512)}, s32[384]{0:T(512)S(1)}) sort(s32[384]{0:T(512)S(1)} %slice_reduce_fusion, s32[384]{0:T(512)S(1)} %iota.4), dimensions={0}, to_apply=%region_0.1 | sort | flops 3456 | bytes 6144 | tf_op jit(solution)/shard_map/jit(argsort)/sort | solution.py:171
  5.3 1.7 %gather_fusion = bf16[384,8,128]{2,1,0:T(8,128)(2,1)S(1)} fusion(bf16[8,384,128]{2,0,1:T(8,128)(2,1)S(1)} %bitcast.14, s32[1024]{0:T(1024)S(1)} %pad_clamp_fusion), kind=kCustom, calls=%fused_computation | custom fusion | bytes 1574400 | tf_op jit(solution)/shard_map/jit(_take)/gather | solution.py:172
  7.3 32.9 %all_to_all.16 = bf16[8,64,768]{2,0,1:T(8,128)(2,1)S(1)} all-to-all(bf16[8,64,768]{2,0,1:T(8,128)(2,1)S(1)} %broadcast_select_fusion), channel_id=1, replica_groups=mesh['region'=64,'orb'=4] {'region'}, dimensions={1} | all-to-all | bytes 1572864 | tf_op jit(solution)/shard_map/all_to_all | solution.py:173
  40.2 3.8 %collective-permute-start = (bf16[512,768]{1,0:T(8,128)(2,1)S(1)}, bf16[512,768]{1,0:T(8,128)(2,1)}, u32[]{:S(2)}, u32[]{:S(2)}) collective-permute-start(bf16[512,768]{1,0:T(8,128)(2,1)S(1)} %bitcast.15), channel_id=1, source_target_pairs={{0,6},{1,7},{2,4},{3,5},{4,10},{5,11},{6,8},{7,9},{8,14},{9,15},{1... | collective-permute-start | bytes 2359304 | tf_op jit(solution)/shard_map/ppermute | solution.py:20
  44.3 2.3 %copy-done.1 = bf16[1,4,768,768]{3,2,1,0:T(8,128)(2,1)S(1)} copy-done((bf16[1,4,768,768]{3,2,1,0:T(8,128)(2,1)S(1)}, bf16[1,4,768,768]{3,2,1,0:T(8,128)(2,1)}, u32[]{:S(2)}) %copy-start.1) | copy-done | bytes 4718616
  46.6 0.6 away.1
  47.2 12.5 %collective-permute-done.refs_0_.refs_2_ = bf16[512,768]{1,0:T(8,128)(2,1)} collective-permute-done((bf16[512,768]{1,0:T(8,128)(2,1)S(1)}, bf16[512,768]{1,0:T(8,128)(2,1)}, u32[]{:S(2)}, u32[]{:S(2)}) %collective-permute-start) | collective-permute-done | bytes 786464 | tf_op jit(solution)/shard_map/ppermute | solution.py:20
  59.8 2.2 %collective-permute-done.1.refs_2_.refs_6_.refs_0_.own = bf16[512,768]{1,0:T(8,128)(2,1)S(1)} collective-permute-done((bf16[512,768]{1,0:T(8,128)(2,1)S(1)}, bf16[512,768]{1,0:T(8,128)(2,1)S(1)}, u32[]{:S(2)}, u32[]{:S(2)}) %collective-permute-start.1) | collective-permute-done | bytes 786464 | tf_op jit(solution)/shard_map/ppermute | solution.py:20
  62.0 3.4 %collective-permute-done.2.refs_2_.ahead.refs_4_ = bf16[512,768]{1,0:T(8,128)(2,1)} collective-permute-done((bf16[512,768]{1,0:T(8,128)(2,1)S(1)}, bf16[512,768]{1,0:T(8,128)(2,1)}, u32[]{:S(2)}, u32[]{:S(2)}) %collective-permute-start.2) | collective-permute-done | bytes 786464 | tf_op jit(solution)/shard_map/ppermute | solution.py:20
  65.9 1.8 %collective-permute-start.4 = (bf16[512,768]{1,0:T(8,128)(2,1)}, bf16[512,768]{1,0:T(8,128)(2,1)S(1)}, u32[]{:S(2)}, u32[]{:S(2)}) collective-permute-start(bf16[512,768]{1,0:T(8,128)(2,1)} %collective-permute-done.refs_0_.refs_2_), channel_id=1, source_target_pairs={{0,2},{1,3},{2,0},{3,1},{4,6},{5,7},{6,4},{7,5},{8,10},{9,11},{10,... | collective-permute-start | bytes 2359304 | tf_op jit(solution)/shard_map/ppermute | solution.py:20
  67.7 1.0 collective-permute-done.6.refs_3_.refs_7_.refs_1_
  68.8 2.7 %collective-permute-start.10 = (bf16[768,768]{1,0:T(8,128)(2,1)S(1)}, bf16[768,768]{1,0:T(8,128)(2,1)S(1)}, u32[]{:S(2)}, u32[]{:S(2)}) collective-permute-start(bf16[768,768]{1,0:T(8,128)(2,1)S(1)} %away.1), channel_id=1, source_target_pairs={{0,6},{1,7},{2,4},{3,5},{4,10},{5,11},{6,8},{7,9},{8,14},{9,15},{1... | collective-permute-start | bytes 3538952 | tf_op jit(solution)/shard_map/ppermute | solution.py:20
  71.4 2.3 %copy-done.2 = bf16[1,4,768,768]{3,2,1,0:T(8,128)(2,1)S(1)} copy-done((bf16[1,4,768,768]{3,2,1,0:T(8,128)(2,1)S(1)}, bf16[1,4,768,768]{3,2,1,0:T(8,128)(2,1)}, u32[]{:S(2)}) %copy-start.2) | copy-done | bytes 4718616
  73.8 2.0 %gram.6.oo = bf16[384,768]{1,0:T(8,128)(2,1)S(1)} custom-call(s32[4]{0:T(128)S(1)} %pad_add_fusion.scalars, bf16[512,768]{1,0:T(8,128)(2,1)S(1)} %bitcast.19, bf16[512,768]{1,0:T(8,128)(2,1)S(1)} %collective-permute-done.5.refs_1_.refs_5_.refs_3_, bf16[512,768]{1,0:T(8,128)(2,1)S(1)} %collective-permute-done.1.refs_2_.refs_6_.refs_0_.own, ...), custom_call_target="tpu_custom_call" | custom-call | tf_op jit(solution)/shard_map/gram/pallas_call | solution.py:24
  75.8 2.6 %gram.7.refs_4_ = f32[384,768]{1,0:T(8,128)S(1)} custom-call(s32[4]{0:T(128)S(1)} %pad_add_fusion.scalars, bf16[512,768]{1,0:T(8,128)(2,1)} %collective-permute-done.refs_0_.refs_2_, bf16[512,768]{1,0:T(8,128)(2,1)S(1)} %collective-permute-done.7.refs_1_.refs_3_, bf16[512,768]{1,0:T(8,128)(2,1)S(1)} %collective-permute-done.1.refs_2_.refs_6_.refs_0_.own, ...), custom_call_target="tpu_custom_call" | custom-call | tf_op jit(solution)/shard_map/gram/pallas_call | solution.py:24
  78.4 2.5 %gram.8.refs_4_ = f32[384,768]{1,0:T(8,128)S(1)} custom-call(s32[4]{0:T(128)S(1)} %pad_add_fusion.scalars, bf16[512,768]{1,0:T(8,128)(2,1)S(1)} %bitcast.21, bf16[512,768]{1,0:T(8,128)(2,1)S(1)} %collective-permute-done.5.refs_1_.refs_5_.refs_3_, bf16[512,768]{1,0:T(8,128)(2,1)} %collective-permute-done.2.refs_2_.ahead.refs_4_, ...), custom_call_target="tpu_custom_call" | custom-call | tf_op jit(solution)/shard_map/gram/pallas_call | solution.py:24
  80.9 8.3 %collective-permute-done.3.refs_2_.refs_6_.ahead = bf16[512,768]{1,0:T(8,128)(2,1)S(1)} collective-permute-done((bf16[512,768]{1,0:T(8,128)(2,1)S(1)}, bf16[512,768]{1,0:T(8,128)(2,1)S(1)}, u32[]{:S(2)}, u32[]{:S(2)}) %collective-permute-start.3) | collective-permute-done | bytes 786464 | tf_op jit(solution)/shard_map/ppermute | solution.py:20
  89.7 1.8 %collective-permute-done.11.refs_3_.refs_7_ = bf16[512,768]{1,0:T(8,128)(2,1)S(1)} collective-permute-done((bf16[512,768]{1,0:T(8,128)(2,1)S(1)}, bf16[512,768]{1,0:T(8,128)(2,1)S(1)}, u32[]{:S(2)}, u32[]{:S(2)}) %collective-permute-start.11) | collective-permute-done | bytes 786464 | tf_op jit(solution)/shard_map/ppermute | solution.py:20
  91.5 1.4 %gram.9.oa = bf16[384,768]{1,0:T(8,128)(2,1)S(1)} custom-call(s32[4]{0:T(128)S(1)} %pad_add_fusion.scalars, bf16[512,768]{1,0:T(8,128)(2,1)S(1)} %collective-permute-done.1.refs_2_.refs_6_.refs_0_.own, bf16[512,768]{1,0:T(8,128)(2,1)S(1)} %collective-permute-done.6.refs_3_.refs_7_.refs_1_, bf16[512,768]{1,0:T(8,128)(2,1)S(1)} %collective-permute-done.3.refs_2_.refs_6_.ahead, ...), custom_call_target="tpu_custom_call" | custom-call | tf_op jit(solution)/shard_map/gram/pallas_call | solution.py:24
  92.9 5.1 %collective-permute-done.10.refs_5_.refs_8_ = bf16[768,768]{1,0:T(8,128)(2,1)S(1)} collective-permute-done((bf16[768,768]{1,0:T(8,128)(2,1)S(1)}, bf16[768,768]{1,0:T(8,128)(2,1)S(1)}, u32[]{:S(2)}, u32[]{:S(2)}) %collective-permute-start.10) | collective-permute-done | bytes 1179680 | tf_op jit(solution)/shard_map/ppermute | solution.py:20
  98.0 3.3 %gram.11.pa = bf16[384,768]{1,0:T(8,128)(2,1)S(1)} custom-call(s32[4]{0:T(128)S(1)} %pad_add_fusion.scalars, bf16[512,768]{1,0:T(8,128)(2,1)S(1)} %collective-permute-done.4.refs_0_.prev, bf16[512,768]{1,0:T(8,128)(2,1)S(1)} %collective-permute-done.13.refs_1_, bf16[512,768]{1,0:T(8,128)(2,1)} %collective-permute-done.refs_0_.refs_2_, ...), custom_call_target="tpu_custom_call" | custom-call | tf_op jit(solution)/shard_map/gram/pallas_call | solution.py:24
  101.9 1.4 gram.10.po
  103.5 2.3 %to_ahead_kernel.1 = bf16[512,768]{1,0:T(8,128)(2,1)S(1)} custom-call(s32[4]{0:T(128)S(1)} %pad_add_fusion.scalars, bf16[512,768]{1,0:T(8,128)(2,1)S(1)} %bitcast.23, bf16[512,768]{1,0:T(8,128)(2,1)S(1)} %collective-permute-done.4.refs_0_.prev, bf16[384,768]{1,0:T(8,128)(2,1)S(1)} %gram.9.oa, bf16[384,768]{1,0:T(8,128)(2,1)S(1)} %collective-permute-done.12.oa_too, ...), custom_call_target="tpu_custom_call" | custom-call | tf_op jit(solution)/shard_map/to_ahead_kernel/pallas_call | solution.py:24
  105.9 4.1 %collective-permute-start.17 = (bf16[512,768]{1,0:T(8,128)(2,1)S(1)}, bf16[512,768]{1,0:T(8,128)(2,1)S(1)}, u32[]{:S(2)}, u32[]{:S(2)}) collective-permute-start(bf16[512,768]{1,0:T(8,128)(2,1)S(1)} %to_ahead_kernel.1), channel_id=1, source_target_pairs={{0,8},{1,9},{2,10},{3,11},{4,12},{5,13},{6,14},{7,15},{8,16},{9,17... | collective-permute-start | bytes 2359304 | tf_op jit(solution)/shard_map/ppermute | solution.py:20
  110.0 2.3 %to_prev_kernel.1 = bf16[512,768]{1,0:T(8,128)(2,1)S(1)} custom-call(s32[4]{0:T(128)S(1)} %pad_add_fusion.scalars, bf16[512,768]{1,0:T(8,128)(2,1)S(1)} %collective-permute-done.1.refs_2_.refs_6_.refs_0_.own, bf16[512,768]{1,0:T(8,128)(2,1)S(1)} %collective-permute-done.3.refs_2_.refs_6_.ahead, bf16[384,768]{1,0:T(8,128)(2,1)S(1)} %gram.10.po, ...), custom_call_target="tpu_custom_call" | custom-call | tf_op jit(solution)/shard_map/to_prev_kernel/pallas_call | solution.py:24
  112.4 3.3 %collective-permute-start.16 = (bf16[512,768]{1,0:T(8,128)(2,1)S(1)}, bf16[512,768]{1,0:T(8,128)(2,1)S(1)}, u32[]{:S(2)}, u32[]{:S(2)}) collective-permute-start(bf16[512,768]{1,0:T(8,128)(2,1)S(1)} %to_prev_kernel.1), channel_id=1, source_target_pairs={{0,254},{1,255},{2,252},{3,253},{4,2},{5,3},{6,0},{7,1},{8,6},{9,7... | collective-permute-start | bytes 2359304 | tf_op jit(solution)/shard_map/ppermute | solution.py:20
  115.7 2.0 %collective-permute-done.9.oo_too = bf16[384,768]{1,0:T(8,128)(2,1)S(1)} collective-permute-done((bf16[384,768]{1,0:T(8,128)(2,1)S(1)}, bf16[384,768]{1,0:T(8,128)(2,1)S(1)}, u32[]{:S(2)}, u32[]{:S(2)}) %collective-permute-start.9) | collective-permute-done | bytes 589856 | tf_op jit(solution)/shard_map/ppermute | solution.py:20
  117.7 4.3 %stay_kernel.1 = f32[512,768]{1,0:T(8,128)S(1)} custom-call(s32[4]{0:T(128)S(1)} %pad_add_fusion.scalars, bf16[512,768]{1,0:T(8,128)(2,1)S(1)} %bitcast.24, bf16[512,768]{1,0:T(8,128)(2,1)} %collective-permute-done.2.refs_2_.ahead.refs_4_, bf16[512,768]{1,0:T(8,128)(2,1)S(1)} %collective-permute-done.4.refs_0_.prev, bf16[384,768]{1,0:T(8,128)(2,1)S(1)} %gram.6.oo, ...), custom_call_target="tpu_custom_call" | custom-call | tf_op jit(solution)/shard_map/stay_kernel/pallas_call | solution.py:24
  122.0 5.4 %collective-permute-done.17 = bf16[512,768]{1,0:T(8,128)(2,1)S(1)} collective-permute-done((bf16[512,768]{1,0:T(8,128)(2,1)S(1)}, bf16[512,768]{1,0:T(8,128)(2,1)S(1)}, u32[]{:S(2)}, u32[]{:S(2)}) %collective-permute-start.17) | collective-permute-done | bytes 786464 | tf_op jit(solution)/shard_map/ppermute | solution.py:20
  127.4 10.0 %collective-permute-done.16 = bf16[512,768]{1,0:T(8,128)(2,1)S(1)} collective-permute-done((bf16[512,768]{1,0:T(8,128)(2,1)S(1)}, bf16[512,768]{1,0:T(8,128)(2,1)S(1)}, u32[]{:S(2)}, u32[]{:S(2)}) %collective-permute-start.16) | collective-permute-done | bytes 786464 | tf_op jit(solution)/shard_map/ppermute | solution.py:20
  137.4 1.4 %add_multiply_fusion = f32[512,768]{1,0:T(8,128)} fusion(bf16[512,768]{1,0:T(8,128)(2,1)S(1)} %collective-permute-done.17, f32[512,768]{1,0:T(8,128)S(1)} %stay_kernel.1, bf16[512,768]{1,0:T(8,128)(2,1)S(1)} %collective-permute-done.16), kind=kLoop, calls=%fused_computation.1 | loop fusion | flops 1966080 | bytes 4718592 | tf_op jit(solution)/shard_map/mul | solution.py:213
  (38 shorter events, 2.7 us)
Async XLA Ops:
  0.0 5.3 %copy-start = (bf16[8,49152]{1,0:T(8,128)(2,1)S(1)}, bf16[8,49152]{1,0:T(8,128)(2,1)}, u32[]{:S(2)}) copy-start(bf16[8,49152]{1,0:T(8,128)(2,1)} %param.4) | copy-start | bytes 2359300
  7.0 37.1 %copy-start.4 = (s32[1,3]{1,0:T(1,128)S(1)}, s32[1,3]{1,0:T(1,128)}, u32[]{:S(2)}) copy-start(s32[1,3]{1,0:T(1,128)} %param.7) | copy-start | bytes 40
  40.2 19.5 %collective-permute-start = (bf16[512,768]{1,0:T(8,128)(2,1)S(1)}, bf16[512,768]{1,0:T(8,128)(2,1)}, u32[]{:S(2)}, u32[]{:S(2)}) collective-permute-start(bf16[512,768]{1,0:T(8,128)(2,1)S(1)} %bitcast.15), channel_id=1, source_target_pairs={{0,6},{1,7},{2,4},{3,5},{4,10},{5,11},{6,8},{7,9},{8,14},{9,15},{1... | collective-permute-start | bytes 2359304 | tf_op jit(solution)/shard_map/ppermute | solution.py:20
  44.0 18.0 %collective-permute-start.1 = (bf16[512,768]{1,0:T(8,128)(2,1)S(1)}, bf16[512,768]{1,0:T(8,128)(2,1)S(1)}, u32[]{:S(2)}, u32[]{:S(2)}) collective-permute-start(bf16[512,768]{1,0:T(8,128)(2,1)S(1)} %bitcast.16), channel_id=1, source_target_pairs={{0,2},{1,3},{2,0},{3,1},{4,6},{5,7},{6,4},{7,5},{8,10},{9,11},{10,... | collective-permute-start | bytes 2359304 | tf_op jit(solution)/shard_map/ppermute | solution.py:20
  44.0 21.4 %collective-permute-start.2 = (bf16[512,768]{1,0:T(8,128)(2,1)S(1)}, bf16[512,768]{1,0:T(8,128)(2,1)}, u32[]{:S(2)}, u32[]{:S(2)}) collective-permute-start(bf16[512,768]{1,0:T(8,128)(2,1)S(1)} %bitcast.17), channel_id=1, source_target_pairs={{0,248},{1,249},{2,250},{3,251},{4,252},{5,253},{6,254},{7,255},{8... | collective-permute-start | bytes 2359304 | tf_op jit(solution)/shard_map/ppermute | solution.py:20
  44.2 21.7 %collective-permute-start.5 = (bf16[512,768]{1,0:T(8,128)(2,1)S(1)}, bf16[512,768]{1,0:T(8,128)(2,1)S(1)}, u32[]{:S(2)}, u32[]{:S(2)}) collective-permute-start(bf16[512,768]{1,0:T(8,128)(2,1)S(1)} %bitcast.18), channel_id=1, source_target_pairs={{0,1},{1,0},{2,3},{3,2},{4,5},{5,4},{6,7},{7,6},{8,9},{9,8},{10,11... | collective-permute-start | bytes 2359304 | tf_op jit(solution)/shard_map/ppermute | solution.py:20
  44.3 2.3 %copy-start.1 = (bf16[1,4,768,768]{3,2,1,0:T(8,128)(2,1)S(1)}, bf16[1,4,768,768]{3,2,1,0:T(8,128)(2,1)}, u32[]{:S(2)}) copy-start(bf16[1,4,768,768]{3,2,1,0:T(8,128)(2,1)} %refs_5_.1) | copy-start | bytes 14155780
  65.4 3.4 %collective-permute-start.6 = (bf16[512,768]{1,0:T(8,128)(2,1)S(1)}, bf16[512,768]{1,0:T(8,128)(2,1)S(1)}, u32[]{:S(2)}, u32[]{:S(2)}) collective-permute-start(bf16[512,768]{1,0:T(8,128)(2,1)S(1)} %collective-permute-done.1.refs_2_.refs_6_.refs_0_.own), channel_id=1, source_target_pairs={{0,1},{1,0},{2,3},{3,2},{4,5},{5,4},{6,7},{7,6},{8,9},{9,8},{10,11... | collective-permute-start | bytes 2359304 | tf_op jit(solution)/shard_map/ppermute | solution.py:20
  65.4 10.4 %collective-permute-start.7 = (bf16[512,768]{1,0:T(8,128)(2,1)}, bf16[512,768]{1,0:T(8,128)(2,1)S(1)}, u32[]{:S(2)}, u32[]{:S(2)}) collective-permute-start(bf16[512,768]{1,0:T(8,128)(2,1)} %collective-permute-done.refs_0_.refs_2_), channel_id=1, source_target_pairs={{0,1},{1,0},{2,3},{3,2},{4,5},{5,4},{6,7},{7,6},{8,9},{9,8},{10,11... | collective-permute-start | bytes 2359304 | tf_op jit(solution)/shard_map/ppermute | solution.py:20
  65.9 12.5 %collective-permute-start.8 = (bf16[512,768]{1,0:T(8,128)(2,1)}, bf16[512,768]{1,0:T(8,128)(2,1)S(1)}, u32[]{:S(2)}, u32[]{:S(2)}) collective-permute-start(bf16[512,768]{1,0:T(8,128)(2,1)} %collective-permute-done.2.refs_2_.ahead.refs_4_), channel_id=1, source_target_pairs={{0,1},{1,0},{2,3},{3,2},{4,5},{5,4},{6,7},{7,6},{8,9},{9,8},{10,11... | collective-permute-start | bytes 2359304 | tf_op jit(solution)/shard_map/ppermute | solution.py:20
  65.9 23.3 %collective-permute-start.3 = (bf16[512,768]{1,0:T(8,128)(2,1)S(1)}, bf16[512,768]{1,0:T(8,128)(2,1)S(1)}, u32[]{:S(2)}, u32[]{:S(2)}) collective-permute-start(bf16[512,768]{1,0:T(8,128)(2,1)S(1)} %collective-permute-done.1.refs_2_.refs_6_.refs_0_.own), channel_id=1, source_target_pairs={{0,248},{1,249},{2,250},{3,251},{4,252},{5,253},{6,254},{7,255},{8... | collective-permute-start | bytes 2359304 | tf_op jit(solution)/shard_map/ppermute | solution.py:20
  65.9 23.3 %collective-permute-start.4 = (bf16[512,768]{1,0:T(8,128)(2,1)}, bf16[512,768]{1,0:T(8,128)(2,1)S(1)}, u32[]{:S(2)}, u32[]{:S(2)}) collective-permute-start(bf16[512,768]{1,0:T(8,128)(2,1)} %collective-permute-done.refs_0_.refs_2_), channel_id=1, source_target_pairs={{0,2},{1,3},{2,0},{3,1},{4,6},{5,7},{6,4},{7,5},{8,10},{9,11},{10,... | collective-permute-start | bytes 2359304 | tf_op jit(solution)/shard_map/ppermute | solution.py:20
  68.8 29.2 %collective-permute-start.10 = (bf16[768,768]{1,0:T(8,128)(2,1)S(1)}, bf16[768,768]{1,0:T(8,128)(2,1)S(1)}, u32[]{:S(2)}, u32[]{:S(2)}) collective-permute-start(bf16[768,768]{1,0:T(8,128)(2,1)S(1)} %away.1), channel_id=1, source_target_pairs={{0,6},{1,7},{2,4},{3,5},{4,10},{5,11},{6,8},{7,9},{8,14},{9,15},{1... | collective-permute-start | bytes 3538952 | tf_op jit(solution)/shard_map/ppermute | solution.py:20
  71.4 2.3 %copy-start.2 = (bf16[1,4,768,768]{3,2,1,0:T(8,128)(2,1)S(1)}, bf16[1,4,768,768]{3,2,1,0:T(8,128)(2,1)}, u32[]{:S(2)}) copy-start(bf16[1,4,768,768]{3,2,1,0:T(8,128)(2,1)} %refs_5_.1) | copy-start | bytes 14155780
  75.8 15.7 %copy-start.3 = (bf16[1,4,768,768]{3,2,1,0:T(8,128)(2,1)S(1)}, bf16[1,4,768,768]{3,2,1,0:T(8,128)(2,1)}, u32[]{:S(2)}) copy-start(bf16[1,4,768,768]{3,2,1,0:T(8,128)(2,1)} %refs_5_.1) | copy-start | bytes 14155780
  89.2 2.3 %collective-permute-start.11 = (bf16[512,768]{1,0:T(8,128)(2,1)S(1)}, bf16[512,768]{1,0:T(8,128)(2,1)S(1)}, u32[]{:S(2)}, u32[]{:S(2)}) collective-permute-start(bf16[512,768]{1,0:T(8,128)(2,1)S(1)} %collective-permute-done.3.refs_2_.refs_6_.ahead), channel_id=1, source_target_pairs={{0,1},{1,0},{2,3},{3,2},{4,5},{5,4},{6,7},{7,6},{8,9},{9,8},{10,11... | collective-permute-start | bytes 2359304 | tf_op jit(solution)/shard_map/ppermute | solution.py:20
  89.2 8.8 %collective-permute-start.13 = (bf16[512,768]{1,0:T(8,128)(2,1)S(1)}, bf16[512,768]{1,0:T(8,128)(2,1)S(1)}, u32[]{:S(2)}, u32[]{:S(2)}) collective-permute-start(bf16[512,768]{1,0:T(8,128)(2,1)S(1)} %collective-permute-done.4.refs_0_.prev), channel_id=1, source_target_pairs={{0,1},{1,0},{2,3},{3,2},{4,5},{5,4},{6,7},{7,6},{8,9},{9,8},{10,11... | collective-permute-start | bytes 2359304 | tf_op jit(solution)/shard_map/ppermute | solution.py:20
  98.0 5.4 %collective-permute-start.12 = (bf16[384,768]{1,0:T(8,128)(2,1)S(1)}, bf16[384,768]{1,0:T(8,128)(2,1)S(1)}, u32[]{:S(2)}, u32[]{:S(2)}) collective-permute-start(bf16[384,768]{1,0:T(8,128)(2,1)S(1)} %gram.9.oa), channel_id=1, source_target_pairs={{0,1},{1,0},{2,3},{3,2},{4,5},{5,4},{6,7},{7,6},{8,9},{9,8},{10,11... | collective-permute-start | bytes 1769480 | tf_op jit(solution)/shard_map/ppermute | solution.py:20
  101.3 2.2 %collective-permute-start.15 = (bf16[384,768]{1,0:T(8,128)(2,1)S(1)}, bf16[384,768]{1,0:T(8,128)(2,1)S(1)}, u32[]{:S(2)}, u32[]{:S(2)}) collective-permute-start(bf16[384,768]{1,0:T(8,128)(2,1)S(1)} %gram.11.pa), channel_id=1, source_target_pairs={{0,1},{1,0},{2,3},{3,2},{4,5},{5,4},{6,7},{7,6},{8,9},{9,8},{10,11... | collective-permute-start | bytes 1769480 | tf_op jit(solution)/shard_map/ppermute | solution.py:20
  103.3 6.7 %collective-permute-start.14 = (bf16[384,768]{1,0:T(8,128)(2,1)S(1)}, bf16[384,768]{1,0:T(8,128)(2,1)S(1)}, u32[]{:S(2)}, u32[]{:S(2)}) collective-permute-start(bf16[384,768]{1,0:T(8,128)(2,1)S(1)} %gram.10.po), channel_id=1, source_target_pairs={{0,1},{1,0},{2,3},{3,2},{4,5},{5,4},{6,7},{7,6},{8,9},{9,8},{10,11... | collective-permute-start | bytes 1769480 | tf_op jit(solution)/shard_map/ppermute | solution.py:20
  105.9 21.5 %collective-permute-start.17 = (bf16[512,768]{1,0:T(8,128)(2,1)S(1)}, bf16[512,768]{1,0:T(8,128)(2,1)S(1)}, u32[]{:S(2)}, u32[]{:S(2)}) collective-permute-start(bf16[512,768]{1,0:T(8,128)(2,1)S(1)} %to_ahead_kernel.1), channel_id=1, source_target_pairs={{0,8},{1,9},{2,10},{3,11},{4,12},{5,13},{6,14},{7,15},{8,16},{9,17... | collective-permute-start | bytes 2359304 | tf_op jit(solution)/shard_map/ppermute | solution.py:20
  112.4 25.0 %collective-permute-start.16 = (bf16[512,768]{1,0:T(8,128)(2,1)S(1)}, bf16[512,768]{1,0:T(8,128)(2,1)S(1)}, u32[]{:S(2)}, u32[]{:S(2)}) collective-permute-start(bf16[512,768]{1,0:T(8,128)(2,1)S(1)} %to_prev_kernel.1), channel_id=1, source_target_pairs={{0,254},{1,255},{2,252},{3,253},{4,2},{5,3},{6,0},{7,1},{8,6},{9,7... | collective-permute-start | bytes 2359304 | tf_op jit(solution)/shard_map/ppermute | solution.py:20
  115.6 2.0 %collective-permute-start.9 = (bf16[384,768]{1,0:T(8,128)(2,1)S(1)}, bf16[384,768]{1,0:T(8,128)(2,1)S(1)}, u32[]{:S(2)}, u32[]{:S(2)}) collective-permute-start(bf16[384,768]{1,0:T(8,128)(2,1)S(1)} %gram.6.oo), channel_id=1, source_target_pairs={{0,1},{1,0},{2,3},{3,2},{4,5},{5,4},{6,7},{7,6},{8,9},{9,8},{10,11... | collective-permute-start | bytes 1769480 | tf_op jit(solution)/shard_map/ppermute | solution.py:20

commit v3 on v2

--- a/solution.py
+++ b/solution.py
@@ -85,13 +85,15 @@
     if partial is not None:
         operands.append(partial)
         specs.append(whole((half, points)))
+    weight = None
     if block is not None:
         operands.append(block)
         if block.ndim == 4:
+            weight = k
             specs.append(pl.BlockSpec((1, 1, half, points), lambda i, s: (0, k, s[0], 0)))
         else:
+            weight = 0
             specs.append(pl.BlockSpec((half, points), lambda i, s: (k, 0)))
-    weight = None if block is None else k if block.ndim == 4 else 0
     return call(
         functools.partial(gram_kernel, len(lefts), weight),
         scalars,
@@ -111,6 +113,7 @@
 
 def away(scalars, coulomb):
     points = coulomb.shape[3]
+    coulomb = pltpu.with_memory_space_constraint(coulomb, pltpu.HBM)
 
     def block(k):
         return pl.BlockSpec((1, 1, points // 2, points), lambda i, s: (0, k, s[0], 0))
@@ -160,17 +163,47 @@
     )
 
 
+def group_kernel(scalars, order, orbitals, out):
+    bricks = out.shape[2] // TILE
+    for region in range(out.shape[0]):
+        for brick in range(bricks):
+            start = pl.multiple_of(order[region * bricks + brick] * TILE, TILE)
+            out[region, :, brick * TILE : (brick + 1) * TILE] = orbitals[:, pl.ds(start, TILE)]
+
+
+def grouped_by_region(scalars, order, orbitals, points):
+    shape = (orbitals.shape[1] // points, orbitals.shape[0], points)
+    return pl.pallas_call(
+        group_kernel,
+        grid_spec=pltpu.PrefetchScalarGridSpec(
+            num_scalar_prefetch=2,
+            grid=(1,),
+            in_specs=[pl.BlockSpec(orbitals.shape, lambda i, s, o: (0, 0))],
+            out_specs=pl.BlockSpec(shape, lambda i, s, o: (0, 0, 0)),
+        ),
+        out_shape=jax.ShapeDtypeStruct(shape, orbitals.dtype),
+        compiler_params=pltpu.CompilerParams(vmem_limit_bytes=24 * 2**20),
+        cost_estimate=pl.CostEstimate(flops=0, bytes_accessed=0, transcendentals=0),
+        name="group",
+    )(scalars, order, orbitals)
+
+
 def per_device(orbitals, point_region, coulomb, pair_mask):
-    count = orbitals.shape[0]
-    npoints = orbitals.shape[1]
-    bricks = npoints // TILE
+    bricks = orbitals.shape[1] // TILE
     core = lax.axis_index("orb") % 2
     scalars = jnp.concatenate([core[None].astype(jnp.int32), pair_mask[0]])
 
     brick_region = point_region.reshape(bricks, TILE)[:, 0]
-    order = jnp.argsort(brick_region, stable=True)
-    grouped = jnp.take(orbitals.reshape(count, bricks, TILE), order, axis=1).reshape(count, npoints)
-    own = lax.all_to_all(grouped, "region", split_axis=1, concat_axis=0, tiled=True)
+    region = jnp.arange(bricks, dtype=jnp.int32)
+    before = (brick_region[None, :] < brick_region[:, None]) | (
+        (brick_region[None, :] == brick_region[:, None]) & (region[None, :] < region[:, None])
+    )
+    rank = jnp.sum(before.astype(jnp.int32), axis=1)
+    order = jnp.sum(jnp.where(rank[:, None] == region[None, :], region[:, None], 0), axis=0)
+    grouped = grouped_by_region(scalars, order, orbitals, coulomb.shape[2])
+    own = lax.all_to_all(grouped, "region", split_axis=0, concat_axis=0, tiled=True)
+    own = own.reshape(-1, coulomb.shape[2])
+
     def beside(block):
         return moved(block, 0, cores=1)
 
@@ -194,7 +227,6 @@
     prev_s, ahead_xs = beside(prev), beside(ahead_x)
     oa = gram(scalars, (own_x, own_xs), (ahead_x, ahead_xs), oa, coulomb, 2)
     behind, oa = lax.optimization_barrier((behind, oa))
-    po = gram(scalars, (prev, prev_s), (own, own_s), po, behind, 0)
     pa = gram(
         scalars,
         (prev, prev_s, prev_x, prev_xs),
@@ -203,12 +235,13 @@
         behind,
         1,
     )
-
-    po, pa, oa, oo = ((p, beside(p)) for p in (po, pa, oa, oo))
+    po = gram(scalars, (prev, prev_s), (own, own_s), po, behind, 0)
+    pa, oa, oo = ((p, beside(p)) for p in (pa, oa, oo))
+    to_ahead = applied(to_ahead_kernel, scalars, (own, prev), (oa, pa), jnp.bfloat16)
+    from_back = moved(to_ahead, 2)
+    po = po, beside(po)
     to_prev = applied(to_prev_kernel, scalars, (own_x, ahead_x), (po, pa), jnp.bfloat16)
     from_next = moved(to_prev, -1, chips=1)
-    to_ahead = applied(to_ahead_kernel, scalars, (own, prev), (oa, pa), jnp.bfloat16)
-    from_back = moved(to_ahead, 2)
     stay = applied(stay_kernel, scalars, (own, ahead, prev), (oo, oa, po), jnp.float32)
     return -0.25 * (stay + from_next.astype(jnp.float32) + from_back.astype(jnp.float32))
 

time: 139 us -> 135 us (0.971)
  local copies, waits for them, and re-layouts: 7.89 us -> 2.21 us
  waiting for transfers between devices: 51.9 us -> 56.8 us
  other arithmetic: 5.47 us -> 2.53 us
  Pallas kernels: 22.8 us -> 20.3 us
  starting transfers between devices: 17.6 us -> 19.6 us
    ppermute x18, waiting for transfers between devices: 51.9 us -> 56.8 us  [moved(): return lax.ppermute(array, ('region', 'orb'), pairs)]
    sort x1 -> x0, other arithmetic: 3.77 us -> none  [per_device(): order = jnp.argsort(brick_region, stable=True)]
    unnamed x11 -> x6, local copies, waits for them, and re-layouts: 4.72 us -> 1.14 us
    pallas_call x10, Pallas kernels: 22.8 us -> 19.2 us  [call(): pl.pallas_call(kernel, grid_spec=pltpu.PrefetchScalarGridSpec(num_scalar_...]
    ppermute x18, starting transfers between devices: 17.6 us -> 19.6 us  [moved(): return lax.ppermute(array, ('region', 'orb'), pairs)]
    gather x1 -> x0, local copies, waits for them, and re-layouts: 1.75 us -> none  [per_device(): jnp.take(orbitals.reshape(count, bricks, TILE), order, axis=1)]
  transfers between devices with their start and end apart: 18 -> 18, of which waited for: 11 -> 10; matrix products, arithmetic and copies ran while one was open for 0% -> 0% of each run, Pallas kernels for 16% -> 14%
where the time goes in v3:
time: 135 us
  waiting for transfers between devices  56.8 us (42%)
  blocking collectives  32.9 us (24%)
  Pallas kernels  20.3 us (15%)
  starting transfers between devices  19.6 us (15%)
  other arithmetic  2.53 us (2%)
  local copies, waits for them, and re-layouts  2.21 us (2%)
    ppermute x18, waiting for transfers between devices, moved(): return lax.ppermute(array, ('region', 'orb'), pairs)  56.8 us
    all_to_all x1, blocking collectives, per_device(): lax.all_to_all(grouped, 'region', split_axis=0, concat_axis=0, tiled=True)  32.9 us
    ppermute x18, starting transfers between devices, moved(): return lax.ppermute(array, ('region', 'orb'), pairs)  19.6 us
    pallas_call x10, Pallas kernels, call(): pl.pallas_call(kernel, grid_spec=pltpu.PrefetchScalarGridSpec(num_scalar_...  19.2 us
  transfers between devices with their start and end apart: 18, of which 10 were waited for; matrix products, arithmetic and copies ran while one was open for 0% of the time, Pallas kernels for 14%

profile of v3, /device:TPU:126, one launch (start us, length us, event | category | flops | bytes accessed | tf_op | source)
XLA Modules:
  0.0 134.5 jit_solution(17793309908144816162)
XLA Ops:
  0.0 1.1 slice_reduce_fusion
  1.5 0.7 pad_add_fusion.scalars
  2.2 1.1 copy-done
  3.3 1.1 group.1
  4.4 32.9 %all_to_all.5 = bf16[64,8,768]{2,1,0:T(8,128)(2,1)S(1)} all-to-all(bf16[64,8,768]{2,1,0:T(8,128)(2,1)S(1)} %group.1), channel_id=1, replica_groups=mesh['region'=64,'orb'=4] {'region'}, dimensions={0} | all-to-all | bytes 1572864 | tf_op jit(solution)/shard_map/all_to_all | solution.py:204
  37.4 3.8 %collective-permute-start = (bf16[512,768]{1,0:T(8,128)(2,1)S(1)}, bf16[512,768]{1,0:T(8,128)(2,1)S(1)}, u32[]{:S(2)}, u32[]{:S(2)}) collective-permute-start(bf16[512,768]{1,0:T(8,128)(2,1)S(1)} %bitcast.6), channel_id=1, source_target_pairs={{0,6},{1,7},{2,4},{3,5},{4,10},{5,11},{6,8},{7,9},{8,14},{9,15},{1... | collective-permute-start | bytes 2359304 | tf_op jit(solution)/shard_map/ppermute | solution.py:20
  41.3 1.9 %away.1 = bf16[768,768]{1,0:T(8,128)(2,1)S(1)} custom-call(s32[4]{0:T(128)S(1)} %pad_add_fusion.scalars, bf16[1,4,768,768]{3,2,1,0:T(8,128)(2,1)} %refs_5_.1, bf16[1,4,768,768]{3,2,1,0:T(8,128)(2,1)} %refs_5_.1), custom_call_target="tpu_custom_call" | custom-call | tf_op jit(solution)/shard_map/away/pallas_call | solution.py:24
  43.2 13.7 %collective-permute-done.refs_0_.refs_2_ = bf16[512,768]{1,0:T(8,128)(2,1)S(1)} collective-permute-done((bf16[512,768]{1,0:T(8,128)(2,1)S(1)}, bf16[512,768]{1,0:T(8,128)(2,1)S(1)}, u32[]{:S(2)}, u32[]{:S(2)}) %collective-permute-start) | collective-permute-done | bytes 786464 | tf_op jit(solution)/shard_map/ppermute | solution.py:20
  56.9 2.2 %collective-permute-done.1.refs_2_.refs_6_.refs_0_.own = bf16[512,768]{1,0:T(8,128)(2,1)S(1)} collective-permute-done((bf16[512,768]{1,0:T(8,128)(2,1)S(1)}, bf16[512,768]{1,0:T(8,128)(2,1)S(1)}, u32[]{:S(2)}, u32[]{:S(2)}) %collective-permute-start.1) | collective-permute-done | bytes 786464 | tf_op jit(solution)/shard_map/ppermute | solution.py:20
  59.1 3.3 %collective-permute-done.2.refs_2_.ahead.refs_4_ = bf16[512,768]{1,0:T(8,128)(2,1)S(1)} collective-permute-done((bf16[512,768]{1,0:T(8,128)(2,1)S(1)}, bf16[512,768]{1,0:T(8,128)(2,1)S(1)}, u32[]{:S(2)}, u32[]{:S(2)}) %collective-permute-start.2) | collective-permute-done | bytes 786464 | tf_op jit(solution)/shard_map/ppermute | solution.py:20
  62.9 1.8 %collective-permute-start.4 = (bf16[512,768]{1,0:T(8,128)(2,1)S(1)}, bf16[512,768]{1,0:T(8,128)(2,1)S(1)}, u32[]{:S(2)}, u32[]{:S(2)}) collective-permute-start(bf16[512,768]{1,0:T(8,128)(2,1)S(1)} %collective-permute-done.refs_0_.refs_2_), channel_id=1, source_target_pairs={{0,2},{1,3},{2,0},{3,1},{4,6},{5,7},{6,4},{7,5},{8,10},{9,11},{10,... | collective-permute-start | bytes 2359304 | tf_op jit(solution)/shard_map/ppermute | solution.py:20
  64.8 3.7 %collective-permute-start.10 = (bf16[768,768]{1,0:T(8,128)(2,1)S(1)}, bf16[768,768]{1,0:T(8,128)(2,1)S(1)}, u32[]{:S(2)}, u32[]{:S(2)}) collective-permute-start(bf16[768,768]{1,0:T(8,128)(2,1)S(1)} %away.1), channel_id=1, source_target_pairs={{0,6},{1,7},{2,4},{3,5},{4,10},{5,11},{6,8},{7,9},{8,14},{9,15},{1... | collective-permute-start | bytes 3538952 | tf_op jit(solution)/shard_map/ppermute | solution.py:20
  68.5 2.0 %gram.6.oo = bf16[384,768]{1,0:T(8,128)(2,1)S(1)} custom-call(s32[4]{0:T(128)S(1)} %pad_add_fusion.scalars, bf16[512,768]{1,0:T(8,128)(2,1)S(1)} %bitcast.10, bf16[512,768]{1,0:T(8,128)(2,1)S(1)} %collective-permute-done.5.refs_1_.refs_5_.refs_3_, bf16[512,768]{1,0:T(8,128)(2,1)S(1)} %collective-permute-done.1.refs_2_.refs_6_.refs_0_.own, ...), custom_call_target="tpu_custom_call" | custom-call | tf_op jit(solution)/shard_map/gram/pallas_call | solution.py:24
  70.5 1.4 %gram.7.refs_4_ = f32[384,768]{1,0:T(8,128)S(1)} custom-call(s32[4]{0:T(128)S(1)} %pad_add_fusion.scalars, bf16[512,768]{1,0:T(8,128)(2,1)S(1)} %collective-permute-done.refs_0_.refs_2_, bf16[512,768]{1,0:T(8,128)(2,1)S(1)} %collective-permute-done.7.refs_1_.refs_3_, bf16[512,768]{1,0:T(8,128)(2,1)S(1)} %collective-permute-done.1.refs_2_.refs_6_.refs_0_.own, ...), custom_call_target="tpu_custom_call" | custom-call | tf_op jit(solution)/shard_map/gram/pallas_call | solution.py:24
  71.9 1.4 %gram.8.refs_4_ = f32[384,768]{1,0:T(8,128)S(1)} custom-call(s32[4]{0:T(128)S(1)} %pad_add_fusion.scalars, bf16[512,768]{1,0:T(8,128)(2,1)S(1)} %bitcast.12, bf16[512,768]{1,0:T(8,128)(2,1)S(1)} %collective-permute-done.5.refs_1_.refs_5_.refs_3_, bf16[512,768]{1,0:T(8,128)(2,1)S(1)} %collective-permute-done.2.refs_2_.ahead.refs_4_, ...), custom_call_target="tpu_custom_call" | custom-call | tf_op jit(solution)/shard_map/gram/pallas_call | solution.py:24
  73.3 12.9 %collective-permute-done.3.refs_2_.refs_6_.ahead = bf16[512,768]{1,0:T(8,128)(2,1)S(1)} collective-permute-done((bf16[512,768]{1,0:T(8,128)(2,1)S(1)}, bf16[512,768]{1,0:T(8,128)(2,1)S(1)}, u32[]{:S(2)}, u32[]{:S(2)}) %collective-permute-start.3) | collective-permute-done | bytes 786464 | tf_op jit(solution)/shard_map/ppermute | solution.py:20
  86.2 0.5 collective-permute-start.13
  86.7 1.8 %collective-permute-done.11.refs_3_.refs_7_ = bf16[512,768]{1,0:T(8,128)(2,1)S(1)} collective-permute-done((bf16[512,768]{1,0:T(8,128)(2,1)S(1)}, bf16[512,768]{1,0:T(8,128)(2,1)S(1)}, u32[]{:S(2)}, u32[]{:S(2)}) %collective-permute-start.11) | collective-permute-done | bytes 786464 | tf_op jit(solution)/shard_map/ppermute | solution.py:20
  88.5 1.4 %gram.9.oa = bf16[384,768]{1,0:T(8,128)(2,1)S(1)} custom-call(s32[4]{0:T(128)S(1)} %pad_add_fusion.scalars, bf16[512,768]{1,0:T(8,128)(2,1)S(1)} %collective-permute-done.1.refs_2_.refs_6_.refs_0_.own, bf16[512,768]{1,0:T(8,128)(2,1)S(1)} %collective-permute-done.6.refs_3_.refs_7_.refs_1_, bf16[512,768]{1,0:T(8,128)(2,1)S(1)} %collective-permute-done.3.refs_2_.refs_6_.ahead, ...), custom_call_target="tpu_custom_call" | custom-call | tf_op jit(solution)/shard_map/gram/pallas_call | solution.py:24
  89.9 4.1 %collective-permute-done.10.refs_5_.refs_8_ = bf16[768,768]{1,0:T(8,128)(2,1)S(1)} collective-permute-done((bf16[768,768]{1,0:T(8,128)(2,1)S(1)}, bf16[768,768]{1,0:T(8,128)(2,1)S(1)}, u32[]{:S(2)}, u32[]{:S(2)}) %collective-permute-start.10) | collective-permute-done | bytes 1179680 | tf_op jit(solution)/shard_map/ppermute | solution.py:20
  94.0 2.0 %gram.11.pa = bf16[384,768]{1,0:T(8,128)(2,1)S(1)} custom-call(s32[4]{0:T(128)S(1)} %pad_add_fusion.scalars, bf16[512,768]{1,0:T(8,128)(2,1)S(1)} %collective-permute-done.4.refs_0_.prev, bf16[512,768]{1,0:T(8,128)(2,1)S(1)} %collective-permute-done.13.refs_1_, bf16[512,768]{1,0:T(8,128)(2,1)S(1)} %collective-permute-done.refs_0_.refs_2_, ...), custom_call_target="tpu_custom_call" | custom-call | tf_op jit(solution)/shard_map/gram/pallas_call | solution.py:24
  96.1 0.6 collective-permute-start.15
  96.7 1.4 %gram.10.po = bf16[384,768]{1,0:T(8,128)(2,1)S(1)} custom-call(s32[4]{0:T(128)S(1)} %pad_add_fusion.scalars, bf16[512,768]{1,0:T(8,128)(2,1)S(1)} %collective-permute-done.4.refs_0_.prev, bf16[512,768]{1,0:T(8,128)(2,1)S(1)} %collective-permute-done.13.refs_1_, bf16[512,768]{1,0:T(8,128)(2,1)S(1)} %bitcast.13, ...), custom_call_target="tpu_custom_call" | custom-call | tf_op jit(solution)/shard_map/gram/pallas_call | solution.py:24
  98.3 2.3 %to_ahead_kernel.1 = bf16[512,768]{1,0:T(8,128)(2,1)S(1)} custom-call(s32[4]{0:T(128)S(1)} %pad_add_fusion.scalars, bf16[512,768]{1,0:T(8,128)(2,1)S(1)} %bitcast.14, bf16[512,768]{1,0:T(8,128)(2,1)S(1)} %collective-permute-done.4.refs_0_.prev, bf16[384,768]{1,0:T(8,128)(2,1)S(1)} %gram.9.oa, bf16[384,768]{1,0:T(8,128)(2,1)S(1)} %collective-permute-done.12.oa_too, ...), custom_call_target="tpu_custom_call" | custom-call | tf_op jit(solution)/shard_map/to_ahead_kernel/pallas_call | solution.py:24
  100.6 5.1 %collective-permute-start.17 = (bf16[512,768]{1,0:T(8,128)(2,1)S(1)}, bf16[512,768]{1,0:T(8,128)(2,1)S(1)}, u32[]{:S(2)}, u32[]{:S(2)}) collective-permute-start(bf16[512,768]{1,0:T(8,128)(2,1)S(1)} %to_ahead_kernel.1), channel_id=1, source_target_pairs={{0,8},{1,9},{2,10},{3,11},{4,12},{5,13},{6,14},{7,15},{8,16},{9,17... | collective-permute-start | bytes 2359304 | tf_op jit(solution)/shard_map/ppermute | solution.py:20
  105.8 2.3 %to_prev_kernel.1 = bf16[512,768]{1,0:T(8,128)(2,1)S(1)} custom-call(s32[4]{0:T(128)S(1)} %pad_add_fusion.scalars, bf16[512,768]{1,0:T(8,128)(2,1)S(1)} %collective-permute-done.1.refs_2_.refs_6_.refs_0_.own, bf16[512,768]{1,0:T(8,128)(2,1)S(1)} %collective-permute-done.3.refs_2_.refs_6_.ahead, bf16[384,768]{1,0:T(8,128)(2,1)S(1)} %gram.10.po, ...), custom_call_target="tpu_custom_call" | custom-call | tf_op jit(solution)/shard_map/to_prev_kernel/pallas_call | solution.py:24
  108.1 3.3 %collective-permute-start.16 = (bf16[512,768]{1,0:T(8,128)(2,1)S(1)}, bf16[512,768]{1,0:T(8,128)(2,1)S(1)}, u32[]{:S(2)}, u32[]{:S(2)}) collective-permute-start(bf16[512,768]{1,0:T(8,128)(2,1)S(1)} %to_prev_kernel.1), channel_id=1, source_target_pairs={{0,254},{1,255},{2,252},{3,253},{4,2},{5,3},{6,0},{7,1},{8,6},{9,7... | collective-permute-start | bytes 2359304 | tf_op jit(solution)/shard_map/ppermute | solution.py:20
  111.4 2.0 %collective-permute-done.9.oo_too = bf16[384,768]{1,0:T(8,128)(2,1)S(1)} collective-permute-done((bf16[384,768]{1,0:T(8,128)(2,1)S(1)}, bf16[384,768]{1,0:T(8,128)(2,1)S(1)}, u32[]{:S(2)}, u32[]{:S(2)}) %collective-permute-start.9) | collective-permute-done | bytes 589856 | tf_op jit(solution)/shard_map/ppermute | solution.py:20
  113.4 3.2 %stay_kernel.1 = f32[512,768]{1,0:T(8,128)S(1)} custom-call(s32[4]{0:T(128)S(1)} %pad_add_fusion.scalars, bf16[512,768]{1,0:T(8,128)(2,1)S(1)} %bitcast.15, bf16[512,768]{1,0:T(8,128)(2,1)S(1)} %collective-permute-done.2.refs_2_.ahead.refs_4_, bf16[512,768]{1,0:T(8,128)(2,1)S(1)} %collective-permute-done.4.refs_0_.prev, bf16[384,768]{1,0:T(8,128)(2,1)S(1)} %gram.6.oo, ...), custom_call_target="tpu_custom_call" | custom-call | tf_op jit(solution)/shard_map/stay_kernel/pallas_call | solution.py:24
  116.6 6.5 %collective-permute-done.17 = bf16[512,768]{1,0:T(8,128)(2,1)S(1)} collective-permute-done((bf16[512,768]{1,0:T(8,128)(2,1)S(1)}, bf16[512,768]{1,0:T(8,128)(2,1)S(1)}, u32[]{:S(2)}, u32[]{:S(2)}) %collective-permute-start.17) | collective-permute-done | bytes 786464 | tf_op jit(solution)/shard_map/ppermute | solution.py:20
  123.1 10.0 %collective-permute-done.16 = bf16[512,768]{1,0:T(8,128)(2,1)S(1)} collective-permute-done((bf16[512,768]{1,0:T(8,128)(2,1)S(1)}, bf16[512,768]{1,0:T(8,128)(2,1)S(1)}, u32[]{:S(2)}, u32[]{:S(2)}) %collective-permute-start.16) | collective-permute-done | bytes 786464 | tf_op jit(solution)/shard_map/ppermute | solution.py:20
  133.1 1.4 %add_multiply_fusion = f32[512,768]{1,0:T(8,128)} fusion(bf16[512,768]{1,0:T(8,128)(2,1)S(1)} %collective-permute-done.17, f32[512,768]{1,0:T(8,128)S(1)} %stay_kernel.1, bf16[512,768]{1,0:T(8,128)(2,1)S(1)} %collective-permute-done.16), kind=kLoop, calls=%fused_computation | loop fusion | flops 1966080 | bytes 4718592 | tf_op jit(solution)/shard_map/mul | solution.py:246
  (28 shorter events, 1.4 us)
Async XLA Ops:
  2.2 1.1 copy-start
  37.4 31.1 %slice-start = ((s8[4718592]{0:T(1024)(128)(4,1)}), s8[4194304]{0:T(1024)(128)(4,1)S(1)}, s32[]{:S(2)}) async-start(s8[4718592]{0:T(1024)(128)(4,1)} %bitcast.4), calls=%async_computation.1 | async-start | bytes 8388608
  37.4 31.1 %slice-start.1 = ((s8[4718592]{0:T(1024)(128)(4,1)}), s8[524288]{0:T(1024)(128)(4,1)S(1)}, s32[]{:S(2)}) async-start(s8[4718592]{0:T(1024)(128)(4,1)} %bitcast.4), calls=%async_computation.2 | async-start | bytes 1048576
  37.4 19.5 %collective-permute-start = (bf16[512,768]{1,0:T(8,128)(2,1)S(1)}, bf16[512,768]{1,0:T(8,128)(2,1)S(1)}, u32[]{:S(2)}, u32[]{:S(2)}) collective-permute-start(bf16[512,768]{1,0:T(8,128)(2,1)S(1)} %bitcast.6), channel_id=1, source_target_pairs={{0,6},{1,7},{2,4},{3,5},{4,10},{5,11},{6,8},{7,9},{8,14},{9,15},{1... | collective-permute-start | bytes 2359304 | tf_op jit(solution)/shard_map/ppermute | solution.py:20
  41.1 18.0 %collective-permute-start.1 = (bf16[512,768]{1,0:T(8,128)(2,1)S(1)}, bf16[512,768]{1,0:T(8,128)(2,1)S(1)}, u32[]{:S(2)}, u32[]{:S(2)}) collective-permute-start(bf16[512,768]{1,0:T(8,128)(2,1)S(1)} %bitcast.7), channel_id=1, source_target_pairs={{0,2},{1,3},{2,0},{3,1},{4,6},{5,7},{6,4},{7,5},{8,10},{9,11},{10,... | collective-permute-start | bytes 2359304 | tf_op jit(solution)/shard_map/ppermute | solution.py:20
  41.1 21.3 %collective-permute-start.2 = (bf16[512,768]{1,0:T(8,128)(2,1)S(1)}, bf16[512,768]{1,0:T(8,128)(2,1)S(1)}, u32[]{:S(2)}, u32[]{:S(2)}) collective-permute-start(bf16[512,768]{1,0:T(8,128)(2,1)S(1)} %bitcast.8), channel_id=1, source_target_pairs={{0,248},{1,249},{2,250},{3,251},{4,252},{5,253},{6,254},{7,255},{8... | collective-permute-start | bytes 2359304 | tf_op jit(solution)/shard_map/ppermute | solution.py:20
  41.3 21.6 %collective-permute-start.5 = (bf16[512,768]{1,0:T(8,128)(2,1)S(1)}, bf16[512,768]{1,0:T(8,128)(2,1)S(1)}, u32[]{:S(2)}, u32[]{:S(2)}) collective-permute-start(bf16[512,768]{1,0:T(8,128)(2,1)S(1)} %bitcast.9), channel_id=1, source_target_pairs={{0,1},{1,0},{2,3},{3,2},{4,5},{5,4},{6,7},{7,6},{8,9},{9,8},{10,11... | collective-permute-start | bytes 2359304 | tf_op jit(solution)/shard_map/ppermute | solution.py:20
  62.4 2.4 %collective-permute-start.6 = (bf16[512,768]{1,0:T(8,128)(2,1)S(1)}, bf16[512,768]{1,0:T(8,128)(2,1)S(1)}, u32[]{:S(2)}, u32[]{:S(2)}) collective-permute-start(bf16[512,768]{1,0:T(8,128)(2,1)S(1)} %collective-permute-done.1.refs_2_.refs_6_.refs_0_.own), channel_id=1, source_target_pairs={{0,1},{1,0},{2,3},{3,2},{4,5},{5,4},{6,7},{7,6},{8,9},{9,8},{10,11... | collective-permute-start | bytes 2359304 | tf_op jit(solution)/shard_map/ppermute | solution.py:20
  62.4 8.1 %collective-permute-start.7 = (bf16[512,768]{1,0:T(8,128)(2,1)S(1)}, bf16[512,768]{1,0:T(8,128)(2,1)S(1)}, u32[]{:S(2)}, u32[]{:S(2)}) collective-permute-start(bf16[512,768]{1,0:T(8,128)(2,1)S(1)} %collective-permute-done.refs_0_.refs_2_), channel_id=1, source_target_pairs={{0,1},{1,0},{2,3},{3,2},{4,5},{5,4},{6,7},{7,6},{8,9},{9,8},{10,11... | collective-permute-start | bytes 2359304 | tf_op jit(solution)/shard_map/ppermute | solution.py:20
  62.9 8.9 %collective-permute-start.8 = (bf16[512,768]{1,0:T(8,128)(2,1)S(1)}, bf16[512,768]{1,0:T(8,128)(2,1)S(1)}, u32[]{:S(2)}, u32[]{:S(2)}) collective-permute-start(bf16[512,768]{1,0:T(8,128)(2,1)S(1)} %collective-permute-done.2.refs_2_.ahead.refs_4_), channel_id=1, source_target_pairs={{0,1},{1,0},{2,3},{3,2},{4,5},{5,4},{6,7},{7,6},{8,9},{9,8},{10,11... | collective-permute-start | bytes 2359304 | tf_op jit(solution)/shard_map/ppermute | solution.py:20
  62.9 23.3 %collective-permute-start.3 = (bf16[512,768]{1,0:T(8,128)(2,1)S(1)}, bf16[512,768]{1,0:T(8,128)(2,1)S(1)}, u32[]{:S(2)}, u32[]{:S(2)}) collective-permute-start(bf16[512,768]{1,0:T(8,128)(2,1)S(1)} %collective-permute-done.1.refs_2_.refs_6_.refs_0_.own), channel_id=1, source_target_pairs={{0,248},{1,249},{2,250},{3,251},{4,252},{5,253},{6,254},{7,255},{8... | collective-permute-start | bytes 2359304 | tf_op jit(solution)/shard_map/ppermute | solution.py:20
  62.9 23.3 %collective-permute-start.4 = (bf16[512,768]{1,0:T(8,128)(2,1)S(1)}, bf16[512,768]{1,0:T(8,128)(2,1)S(1)}, u32[]{:S(2)}, u32[]{:S(2)}) collective-permute-start(bf16[512,768]{1,0:T(8,128)(2,1)S(1)} %collective-permute-done.refs_0_.refs_2_), channel_id=1, source_target_pairs={{0,2},{1,3},{2,0},{3,1},{4,6},{5,7},{6,4},{7,5},{8,10},{9,11},{10,... | collective-permute-start | bytes 2359304 | tf_op jit(solution)/shard_map/ppermute | solution.py:20
  64.8 29.2 %collective-permute-start.10 = (bf16[768,768]{1,0:T(8,128)(2,1)S(1)}, bf16[768,768]{1,0:T(8,128)(2,1)S(1)}, u32[]{:S(2)}, u32[]{:S(2)}) collective-permute-start(bf16[768,768]{1,0:T(8,128)(2,1)S(1)} %away.1), channel_id=1, source_target_pairs={{0,6},{1,7},{2,4},{3,5},{4,10},{5,11},{6,8},{7,9},{8,14},{9,15},{1... | collective-permute-start | bytes 3538952 | tf_op jit(solution)/shard_map/ppermute | solution.py:20
  86.2 2.3 %collective-permute-start.11 = (bf16[512,768]{1,0:T(8,128)(2,1)S(1)}, bf16[512,768]{1,0:T(8,128)(2,1)S(1)}, u32[]{:S(2)}, u32[]{:S(2)}) collective-permute-start(bf16[512,768]{1,0:T(8,128)(2,1)S(1)} %collective-permute-done.3.refs_2_.refs_6_.ahead), channel_id=1, source_target_pairs={{0,1},{1,0},{2,3},{3,2},{4,5},{5,4},{6,7},{7,6},{8,9},{9,8},{10,11... | collective-permute-start | bytes 2359304 | tf_op jit(solution)/shard_map/ppermute | solution.py:20
  86.2 7.8 %collective-permute-start.13 = (bf16[512,768]{1,0:T(8,128)(2,1)S(1)}, bf16[512,768]{1,0:T(8,128)(2,1)S(1)}, u32[]{:S(2)}, u32[]{:S(2)}) collective-permute-start(bf16[512,768]{1,0:T(8,128)(2,1)S(1)} %collective-permute-done.4.refs_0_.prev), channel_id=1, source_target_pairs={{0,1},{1,0},{2,3},{3,2},{4,5},{5,4},{6,7},{7,6},{8,9},{9,8},{10,11... | collective-permute-start | bytes 2359304 | tf_op jit(solution)/shard_map/ppermute | solution.py:20
  94.0 4.1 %collective-permute-start.12 = (bf16[384,768]{1,0:T(8,128)(2,1)S(1)}, bf16[384,768]{1,0:T(8,128)(2,1)S(1)}, u32[]{:S(2)}, u32[]{:S(2)}) collective-permute-start(bf16[384,768]{1,0:T(8,128)(2,1)S(1)} %gram.9.oa), channel_id=1, source_target_pairs={{0,1},{1,0},{2,3},{3,2},{4,5},{5,4},{6,7},{7,6},{8,9},{9,8},{10,11... | collective-permute-start | bytes 1769480 | tf_op jit(solution)/shard_map/ppermute | solution.py:20
  96.1 2.2 %collective-permute-start.15 = (bf16[384,768]{1,0:T(8,128)(2,1)S(1)}, bf16[384,768]{1,0:T(8,128)(2,1)S(1)}, u32[]{:S(2)}, u32[]{:S(2)}) collective-permute-start(bf16[384,768]{1,0:T(8,128)(2,1)S(1)} %gram.11.pa), channel_id=1, source_target_pairs={{0,1},{1,0},{2,3},{3,2},{4,5},{5,4},{6,7},{7,6},{8,9},{9,8},{10,11... | collective-permute-start | bytes 1769480 | tf_op jit(solution)/shard_map/ppermute | solution.py:20
  98.0 7.7 %collective-permute-start.14 = (bf16[384,768]{1,0:T(8,128)(2,1)S(1)}, bf16[384,768]{1,0:T(8,128)(2,1)S(1)}, u32[]{:S(2)}, u32[]{:S(2)}) collective-permute-start(bf16[384,768]{1,0:T(8,128)(2,1)S(1)} %gram.10.po), channel_id=1, source_target_pairs={{0,1},{1,0},{2,3},{3,2},{4,5},{5,4},{6,7},{7,6},{8,9},{9,8},{10,11... | collective-permute-start | bytes 1769480 | tf_op jit(solution)/shard_map/ppermute | solution.py:20
  100.6 22.5 %collective-permute-start.17 = (bf16[512,768]{1,0:T(8,128)(2,1)S(1)}, bf16[512,768]{1,0:T(8,128)(2,1)S(1)}, u32[]{:S(2)}, u32[]{:S(2)}) collective-permute-start(bf16[512,768]{1,0:T(8,128)(2,1)S(1)} %to_ahead_kernel.1), channel_id=1, source_target_pairs={{0,8},{1,9},{2,10},{3,11},{4,12},{5,13},{6,14},{7,15},{8,16},{9,17... | collective-permute-start | bytes 2359304 | tf_op jit(solution)/shard_map/ppermute | solution.py:20
  108.1 25.0 %collective-permute-start.16 = (bf16[512,768]{1,0:T(8,128)(2,1)S(1)}, bf16[512,768]{1,0:T(8,128)(2,1)S(1)}, u32[]{:S(2)}, u32[]{:S(2)}) collective-permute-start(bf16[512,768]{1,0:T(8,128)(2,1)S(1)} %to_prev_kernel.1), channel_id=1, source_target_pairs={{0,254},{1,255},{2,252},{3,253},{4,2},{5,3},{6,0},{7,1},{8,6},{9,7... | collective-permute-start | bytes 2359304 | tf_op jit(solution)/shard_map/ppermute | solution.py:20
  111.4 2.0 %collective-permute-start.9 = (bf16[384,768]{1,0:T(8,128)(2,1)S(1)}, bf16[384,768]{1,0:T(8,128)(2,1)S(1)}, u32[]{:S(2)}, u32[]{:S(2)}) collective-permute-start(bf16[384,768]{1,0:T(8,128)(2,1)S(1)} %gram.6.oo), channel_id=1, source_target_pairs={{0,1},{1,0},{2,3},{3,2},{4,5},{5,4},{6,7},{7,6},{8,9},{9,8},{10,11... | collective-permute-start | bytes 1769480 | tf_op jit(solution)/shard_map/ppermute | solution.py:20

commit v4 on v3

--- a/solution.py
+++ b/solution.py
@@ -65,7 +65,7 @@
     lefts, rights, rest, out = refs[:count], refs[count : 2 * count], refs[2 * count : -1], refs[-1]
     total = sum(first_rows(left[...], right[...]) for left, right in zip(lefts, rights))
     if weight is None:
-        out[...] = total
+        out[...] = total + rest[0][...] if rest else total
         return
     *partial, block = rest
     if partial:
@@ -85,15 +85,10 @@
     if partial is not None:
         operands.append(partial)
         specs.append(whole((half, points)))
-    weight = None
     if block is not None:
         operands.append(block)
-        if block.ndim == 4:
-            weight = k
-            specs.append(pl.BlockSpec((1, 1, half, points), lambda i, s: (0, k, s[0], 0)))
-        else:
-            weight = 0
-            specs.append(pl.BlockSpec((half, points), lambda i, s: (k, 0)))
+        specs.append(pl.BlockSpec((1, 1, half, points), lambda i, s: (0, k, s[0], 0)))
+    weight = None if block is None else k
     return call(
         functools.partial(gram_kernel, len(lefts), weight),
         scalars,
@@ -105,6 +100,22 @@
     )
 
 
+def screen_kernel(scalars, gram, block, out):
+    out[...] = (gram[...] * block[...].astype(jnp.float32)).astype(out.dtype)
+
+
+def screened(scalars, gram, blocks, k):
+    return call(
+        screen_kernel,
+        scalars,
+        (gram, blocks),
+        [whole(gram.shape), pl.BlockSpec(gram.shape, lambda i, s: (k, 0))],
+        whole(gram.shape),
+        jax.ShapeDtypeStruct(gram.shape, jnp.bfloat16),
+        "screen",
+    )
+
+
 def away_kernel(scalars, one, three, out):
     half = out.shape[0] // 2
     out[:half] = one[0, 0] * scalars[1].astype(out.dtype)
@@ -149,9 +160,7 @@
         out[:, part] += onto_rows(own[...], by_own[...]) + onto_rows(ahead[...], by_ahead[...])
 
 
-def applied(kernel, scalars, orbs, products, dtype):
-    shape = orbs[0].shape
-    operands = (*orbs, *(p for pair in products for p in pair))
+def applied(kernel, scalars, operands, shape, dtype):
     return call(
         kernel,
         scalars,
@@ -214,7 +223,7 @@
 
     later, _ = lax.optimization_barrier((scalars, own))
     sent = away(later, coulomb)
-    prev_x, own_x, ahead, sent = lax.optimization_barrier((prev_x, own_x, ahead, sent))
+    prev_x, sent = lax.optimization_barrier((prev_x, sent))
     behind = moved(sent, 1, chips=1)
     prev = moved(prev_x, 0, chips=1)
     ahead_x = moved(own_x, -2)
@@ -223,26 +232,23 @@
     oo = gram(scalars, all_own, all_own, None, coulomb, 0)
     po = gram(scalars, (prev_x, prev_xs), (own_x, own_xs))
     oa = gram(scalars, (own, own_s), (ahead, ahead_s))
-    ahead_x, prev, oo, po, oa = lax.optimization_barrier((ahead_x, prev, oo, po, oa))
+    ahead_x, prev, oo = lax.optimization_barrier((ahead_x, prev, own_xs))[:2] + (oo,)
     prev_s, ahead_xs = beside(prev), beside(ahead_x)
     oa = gram(scalars, (own_x, own_xs), (ahead_x, ahead_xs), oa, coulomb, 2)
-    behind, oa = lax.optimization_barrier((behind, oa))
-    pa = gram(
-        scalars,
-        (prev, prev_s, prev_x, prev_xs),
-        (ahead, ahead_s, ahead_x, ahead_xs),
-        None,
-        behind,
-        1,
-    )
-    po = gram(scalars, (prev, prev_s), (own, own_s), po, behind, 0)
-    pa, oa, oo = ((p, beside(p)) for p in (pa, oa, oo))
-    to_ahead = applied(to_ahead_kernel, scalars, (own, prev), (oa, pa), jnp.bfloat16)
+    pa = gram(scalars, (prev, prev_s, prev_x, prev_xs), (ahead, ahead_s, ahead_x, ahead_xs))
+    po = gram(scalars, (prev, prev_s), (own, own_s), po)
+    shape = own.shape
+    behind, pa, po, _ = lax.optimization_barrier((behind, pa, po, oa))
+    shape = own.shape
+    oo, oa = ((p, beside(p)) for p in (oo, oa))
+    pa = screened(scalars, pa, behind, 1)
+    po = screened(scalars, po, behind, 0)
+    pa, po = ((p, beside(p)) for p in (pa, po))
+    to_ahead = applied(to_ahead_kernel, scalars, (own, prev, *oa, *pa), shape, jnp.bfloat16)
     from_back = moved(to_ahead, 2)
-    po = po, beside(po)
-    to_prev = applied(to_prev_kernel, scalars, (own_x, ahead_x), (po, pa), jnp.bfloat16)
+    to_prev = applied(to_prev_kernel, scalars, (own_x, ahead_x, *po, *pa), shape, jnp.bfloat16)
     from_next = moved(to_prev, -1, chips=1)
-    stay = applied(stay_kernel, scalars, (own, ahead, prev), (oo, oa, po), jnp.float32)
+    stay = applied(stay_kernel, scalars, (own, ahead, prev, *oo, *oa, *po), shape, jnp.float32)
     return -0.25 * (stay + from_next.astype(jnp.float32) + from_back.astype(jnp.float32))
 
 

time: 135 us -> 130 us (0.963)
  waiting for transfers between devices: 56.8 us -> 50 us
    ppermute x18, waiting for transfers between devices: 56.8 us -> 50 us  [moved(): return lax.ppermute(array, ('region', 'orb'), pairs)]
    pallas_call x10 -> x12, Pallas kernels: 19.2 us -> 20.5 us  [call(): pl.pallas_call(kernel, grid_spec=pltpu.PrefetchScalarGridSpec(num_scalar_...]
  transfers between devices with their start and end apart: 18 -> 18, of which waited for: 10 -> 10; matrix products, arithmetic and copies ran while one was open for 0% -> 0% of each run, Pallas kernels for 14% -> 16%
where the time goes in v4:
time: 130 us; the launch traced here: 128 us
  waiting for transfers between devices  50 us (38%)
  blocking collectives  33.2 us (26%)
  Pallas kernels  21.6 us (17%)
  starting transfers between devices  18.6 us (14%)
  other arithmetic  2.53 us (2%)
  local copies, waits for them, and re-layouts  2.21 us (2%)
    ppermute x18, waiting for transfers between devices, moved(): return lax.ppermute(array, ('region', 'orb'), pairs)  50 us
    all_to_all x1, blocking collectives, per_device(): lax.all_to_all(grouped, 'region', split_axis=0, concat_axis=0, tiled=True)  33.2 us
    pallas_call x12, Pallas kernels, call(): pl.pallas_call(kernel, grid_spec=pltpu.PrefetchScalarGridSpec(num_scalar_...  20.5 us
    ppermute x18, starting transfers between devices, moved(): return lax.ppermute(array, ('region', 'orb'), pairs)  18.6 us
  transfers between devices with their start and end apart: 18, of which 10 were waited for; matrix products, arithmetic and copies ran while one was open for 0% of the time, Pallas kernels for 16%

profile of v4, /device:TPU:126, one launch (start us, length us, event | category | flops | bytes accessed | tf_op | source)
XLA Modules:
  0.0 128.3 jit_solution(10484480823889523781)
XLA Ops:
  0.0 1.1 slice_reduce_fusion
  1.5 0.7 pad_add_fusion.scalars
  2.2 1.1 copy-done
  3.3 1.1 group.1
  4.4 33.2 %all_to_all.5 = bf16[64,8,768]{2,1,0:T(8,128)(2,1)S(1)} all-to-all(bf16[64,8,768]{2,1,0:T(8,128)(2,1)S(1)} %group.1), channel_id=1, replica_groups=mesh['region'=64,'orb'=4] {'region'}, dimensions={0} | all-to-all | bytes 1572864 | tf_op jit(solution)/shard_map/all_to_all | solution.py:213
  37.6 3.8 %collective-permute-start.3 = (bf16[512,768]{1,0:T(8,128)(2,1)S(1)}, bf16[512,768]{1,0:T(8,128)(2,1)S(1)}, u32[]{:S(2)}, u32[]{:S(2)}) collective-permute-start(bf16[512,768]{1,0:T(8,128)(2,1)S(1)} %bitcast.6), channel_id=1, source_target_pairs={{0,6},{1,7},{2,4},{3,5},{4,10},{5,11},{6,8},{7,9},{8,14},{9,15},{1... | collective-permute-start | bytes 2359304 | tf_op jit(solution)/shard_map/ppermute | solution.py:20
  41.6 1.9 %away.1 = bf16[768,768]{1,0:T(8,128)(2,1)S(1)} custom-call(s32[4]{0:T(128)S(1)} %pad_add_fusion.scalars, bf16[1,4,768,768]{3,2,1,0:T(8,128)(2,1)} %refs_5_.1, bf16[1,4,768,768]{3,2,1,0:T(8,128)(2,1)} %refs_5_.1), custom_call_target="tpu_custom_call" | custom-call | tf_op jit(solution)/shard_map/away/pallas_call | solution.py:24
  43.5 13.7 %collective-permute-done.3.refs_2_.refs_0_ = bf16[512,768]{1,0:T(8,128)(2,1)S(1)} collective-permute-done((bf16[512,768]{1,0:T(8,128)(2,1)S(1)}, bf16[512,768]{1,0:T(8,128)(2,1)S(1)}, u32[]{:S(2)}, u32[]{:S(2)}) %collective-permute-start.3) | collective-permute-done | bytes 786464 | tf_op jit(solution)/shard_map/ppermute | solution.py:20
  57.2 2.2 %collective-permute-done.1.refs_2_.refs_6_.refs_0_.own = bf16[512,768]{1,0:T(8,128)(2,1)S(1)} collective-permute-done((bf16[512,768]{1,0:T(8,128)(2,1)S(1)}, bf16[512,768]{1,0:T(8,128)(2,1)S(1)}, u32[]{:S(2)}, u32[]{:S(2)}) %collective-permute-start.1) | collective-permute-done | bytes 786464 | tf_op jit(solution)/shard_map/ppermute | solution.py:20
  60.2 2.5 %collective-permute-done.refs_2_.refs_4_.ahead = bf16[512,768]{1,0:T(8,128)(2,1)S(1)} collective-permute-done((bf16[512,768]{1,0:T(8,128)(2,1)S(1)}, bf16[512,768]{1,0:T(8,128)(2,1)S(1)}, u32[]{:S(2)}, u32[]{:S(2)}) %collective-permute-start) | collective-permute-done | bytes 786464 | tf_op jit(solution)/shard_map/ppermute | solution.py:20
  62.7 3.0 %collective-permute-start.11 = (bf16[768,768]{1,0:T(8,128)(2,1)S(1)}, bf16[768,768]{1,0:T(8,128)(2,1)S(1)}, u32[]{:S(2)}, u32[]{:S(2)}) collective-permute-start(bf16[768,768]{1,0:T(8,128)(2,1)S(1)} %away.1), channel_id=1, source_target_pairs={{0,6},{1,7},{2,4},{3,5},{4,10},{5,11},{6,8},{7,9},{8,14},{9,15},{1... | collective-permute-start | bytes 3538952 | tf_op jit(solution)/shard_map/ppermute | solution.py:20
  65.7 14.0 %collective-permute-done.2.refs_2_.refs_6_.ahead = bf16[512,768]{1,0:T(8,128)(2,1)S(1)} collective-permute-done((bf16[512,768]{1,0:T(8,128)(2,1)S(1)}, bf16[512,768]{1,0:T(8,128)(2,1)S(1)}, u32[]{:S(2)}, u32[]{:S(2)}) %collective-permute-start.2) | collective-permute-done | bytes 786464 | tf_op jit(solution)/shard_map/ppermute | solution.py:20
  80.8 1.4 %gram.10.refs_4_ = f32[384,768]{1,0:T(8,128)S(1)} custom-call(s32[4]{0:T(128)S(1)} %pad_add_fusion.scalars, bf16[512,768]{1,0:T(8,128)(2,1)S(1)} %collective-permute-done.3.refs_2_.refs_0_, bf16[512,768]{1,0:T(8,128)(2,1)S(1)} %collective-permute-done.13.refs_3_.refs_1_, bf16[512,768]{1,0:T(8,128)(2,1)S(1)} %collective-permute-done.1.refs_2_.refs_6_.refs_0_.own, ...), custom_call_target="tpu_custom_call" | custom-call | tf_op jit(solution)/shard_map/gram/pallas_call | solution.py:24
  82.1 1.0 collective-permute-done.9.refs_3_.refs_5_
  83.1 1.4 %gram.7.refs_4_ = f32[384,768]{1,0:T(8,128)S(1)} custom-call(s32[4]{0:T(128)S(1)} %pad_add_fusion.scalars, bf16[512,768]{1,0:T(8,128)(2,1)S(1)} %bitcast.10, bf16[512,768]{1,0:T(8,128)(2,1)S(1)} %collective-permute-done.6.refs_1_.refs_5_.refs_3_, bf16[512,768]{1,0:T(8,128)(2,1)S(1)} %collective-permute-done.refs_2_.refs_4_.ahead, ...), custom_call_target="tpu_custom_call" | custom-call | tf_op jit(solution)/shard_map/gram/pallas_call | solution.py:24
  84.5 1.4 %gram.8.oa = bf16[384,768]{1,0:T(8,128)(2,1)S(1)} custom-call(s32[4]{0:T(128)S(1)} %pad_add_fusion.scalars, bf16[512,768]{1,0:T(8,128)(2,1)S(1)} %collective-permute-done.1.refs_2_.refs_6_.refs_0_.own, bf16[512,768]{1,0:T(8,128)(2,1)S(1)} %collective-permute-done.5.refs_3_.refs_7_.refs_1_, bf16[512,768]{1,0:T(8,128)(2,1)S(1)} %collective-permute-done.2.refs_2_.refs_6_.ahead, ...), custom_call_target="tpu_custom_call" | custom-call | tf_op jit(solution)/shard_map/gram/pallas_call | solution.py:24
  86.4 2.0 %gram.9 = f32[384,768]{1,0:T(8,128)S(1)} custom-call(s32[4]{0:T(128)S(1)} %pad_add_fusion.scalars, bf16[512,768]{1,0:T(8,128)(2,1)S(1)} %collective-permute-done.4.refs_0_.prev, bf16[512,768]{1,0:T(8,128)(2,1)S(1)} %collective-permute-done.12.refs_1_, bf16[512,768]{1,0:T(8,128)(2,1)S(1)} %collective-permute-done.3.refs_2_.refs_0_, ...), custom_call_target="tpu_custom_call" | custom-call | tf_op jit(solution)/shard_map/gram/pallas_call | solution.py:24
  88.4 1.4 %gram.11 = f32[384,768]{1,0:T(8,128)S(1)} custom-call(s32[4]{0:T(128)S(1)} %pad_add_fusion.scalars, bf16[512,768]{1,0:T(8,128)(2,1)S(1)} %collective-permute-done.4.refs_0_.prev, bf16[512,768]{1,0:T(8,128)(2,1)S(1)} %collective-permute-done.12.refs_1_, bf16[512,768]{1,0:T(8,128)(2,1)S(1)} %bitcast.11, ...), custom_call_target="tpu_custom_call" | custom-call | tf_op jit(solution)/shard_map/gram/pallas_call | solution.py:24
  89.8 1.4 %collective-permute-done.11.block = bf16[768,768]{1,0:T(8,128)(2,1)S(1)} collective-permute-done((bf16[768,768]{1,0:T(8,128)(2,1)S(1)}, bf16[768,768]{1,0:T(8,128)(2,1)S(1)}, u32[]{:S(2)}, u32[]{:S(2)}) %collective-permute-start.11) | collective-permute-done | bytes 1179680 | tf_op jit(solution)/shard_map/ppermute | solution.py:20
  91.2 0.6 screen.3.pa
  91.9 0.6 screen.2.po
  93.2 0.8 collective-permute-done.15.pa_too
  93.9 2.3 %to_ahead_kernel.1 = bf16[512,768]{1,0:T(8,128)(2,1)S(1)} custom-call(s32[4]{0:T(128)S(1)} %pad_add_fusion.scalars, bf16[512,768]{1,0:T(8,128)(2,1)S(1)} %bitcast.12, bf16[512,768]{1,0:T(8,128)(2,1)S(1)} %collective-permute-done.4.refs_0_.prev, bf16[384,768]{1,0:T(8,128)(2,1)S(1)} %gram.8.oa, bf16[384,768]{1,0:T(8,128)(2,1)S(1)} %collective-permute-done.10.oa_too, ...), custom_call_target="tpu_custom_call" | custom-call | tf_op jit(solution)/shard_map/to_ahead_kernel/pallas_call | solution.py:24
  96.3 3.5 %collective-permute-start.17 = (bf16[512,768]{1,0:T(8,128)(2,1)S(1)}, bf16[512,768]{1,0:T(8,128)(2,1)S(1)}, u32[]{:S(2)}, u32[]{:S(2)}) collective-permute-start(bf16[512,768]{1,0:T(8,128)(2,1)S(1)} %to_ahead_kernel.1), channel_id=1, source_target_pairs={{0,8},{1,9},{2,10},{3,11},{4,12},{5,13},{6,14},{7,15},{8,16},{9,17... | collective-permute-start | bytes 2359304 | tf_op jit(solution)/shard_map/ppermute | solution.py:20
  99.8 2.3 %to_prev_kernel.1 = bf16[512,768]{1,0:T(8,128)(2,1)S(1)} custom-call(s32[4]{0:T(128)S(1)} %pad_add_fusion.scalars, bf16[512,768]{1,0:T(8,128)(2,1)S(1)} %collective-permute-done.1.refs_2_.refs_6_.refs_0_.own, bf16[512,768]{1,0:T(8,128)(2,1)S(1)} %collective-permute-done.2.refs_2_.refs_6_.ahead, bf16[384,768]{1,0:T(8,128)(2,1)S(1)} %screen.2.po, ...), custom_call_target="tpu_custom_call" | custom-call | tf_op jit(solution)/shard_map/to_prev_kernel/pallas_call | solution.py:24
  102.1 5.1 %collective-permute-start.16 = (bf16[512,768]{1,0:T(8,128)(2,1)S(1)}, bf16[512,768]{1,0:T(8,128)(2,1)S(1)}, u32[]{:S(2)}, u32[]{:S(2)}) collective-permute-start(bf16[512,768]{1,0:T(8,128)(2,1)S(1)} %to_prev_kernel.1), channel_id=1, source_target_pairs={{0,254},{1,255},{2,252},{3,253},{4,2},{5,3},{6,0},{7,1},{8,6},{9,7... | collective-permute-start | bytes 2359304 | tf_op jit(solution)/shard_map/ppermute | solution.py:20
  107.2 2.0 %gram.6.oo = bf16[384,768]{1,0:T(8,128)(2,1)S(1)} custom-call(s32[4]{0:T(128)S(1)} %pad_add_fusion.scalars, bf16[512,768]{1,0:T(8,128)(2,1)S(1)} %bitcast.13, bf16[512,768]{1,0:T(8,128)(2,1)S(1)} %collective-permute-done.6.refs_1_.refs_5_.refs_3_, bf16[512,768]{1,0:T(8,128)(2,1)S(1)} %collective-permute-done.1.refs_2_.refs_6_.refs_0_.own, ...), custom_call_target="tpu_custom_call" | custom-call | tf_op jit(solution)/shard_map/gram/pallas_call | solution.py:24
  109.4 2.0 %collective-permute-done.7.oo_too = bf16[384,768]{1,0:T(8,128)(2,1)S(1)} collective-permute-done((bf16[384,768]{1,0:T(8,128)(2,1)S(1)}, bf16[384,768]{1,0:T(8,128)(2,1)S(1)}, u32[]{:S(2)}, u32[]{:S(2)}) %collective-permute-start.7) | collective-permute-done | bytes 589856 | tf_op jit(solution)/shard_map/ppermute | solution.py:20
  111.3 3.2 %stay_kernel.1 = f32[512,768]{1,0:T(8,128)S(1)} custom-call(s32[4]{0:T(128)S(1)} %pad_add_fusion.scalars, bf16[512,768]{1,0:T(8,128)(2,1)S(1)} %bitcast.15, bf16[512,768]{1,0:T(8,128)(2,1)S(1)} %collective-permute-done.refs_2_.refs_4_.ahead, bf16[512,768]{1,0:T(8,128)(2,1)S(1)} %collective-permute-done.4.refs_0_.prev, bf16[384,768]{1,0:T(8,128)(2,1)S(1)} %gram.6.oo, ...), custom_call_target="tpu_custom_call" | custom-call | tf_op jit(solution)/shard_map/stay_kernel/pallas_call | solution.py:24
  114.5 2.3 %collective-permute-done.17 = bf16[512,768]{1,0:T(8,128)(2,1)S(1)} collective-permute-done((bf16[512,768]{1,0:T(8,128)(2,1)S(1)}, bf16[512,768]{1,0:T(8,128)(2,1)S(1)}, u32[]{:S(2)}, u32[]{:S(2)}) %collective-permute-start.17) | collective-permute-done | bytes 786464 | tf_op jit(solution)/shard_map/ppermute | solution.py:20
  116.8 10.0 %collective-permute-done.16 = bf16[512,768]{1,0:T(8,128)(2,1)S(1)} collective-permute-done((bf16[512,768]{1,0:T(8,128)(2,1)S(1)}, bf16[512,768]{1,0:T(8,128)(2,1)S(1)}, u32[]{:S(2)}, u32[]{:S(2)}) %collective-permute-start.16) | collective-permute-done | bytes 786464 | tf_op jit(solution)/shard_map/ppermute | solution.py:20
  126.9 1.4 %add_multiply_fusion = f32[512,768]{1,0:T(8,128)} fusion(bf16[512,768]{1,0:T(8,128)(2,1)S(1)} %collective-permute-done.17, f32[512,768]{1,0:T(8,128)S(1)} %stay_kernel.1, bf16[512,768]{1,0:T(8,128)(2,1)S(1)} %collective-permute-done.16), kind=kLoop, calls=%fused_computation | loop fusion | flops 1966080 | bytes 4718592 | tf_op jit(solution)/shard_map/mul | solution.py:252
  (30 shorter events, 3.6 us)
Async XLA Ops:
  2.2 1.1 copy-start
  4.4 80.1 %slice-start = ((s8[4718592]{0:T(1024)(128)(4,1)}), s8[4194304]{0:T(1024)(128)(4,1)S(1)}, s32[]{:S(2)}) async-start(s8[4718592]{0:T(1024)(128)(4,1)} %bitcast.4), calls=%async_computation.1 | async-start | bytes 8388608
  37.6 46.9 %slice-start.1 = ((s8[4718592]{0:T(1024)(128)(4,1)}), s8[524288]{0:T(1024)(128)(4,1)S(1)}, s32[]{:S(2)}) async-start(s8[4718592]{0:T(1024)(128)(4,1)} %bitcast.4), calls=%async_computation.2 | async-start | bytes 1048576
  37.6 19.5 %collective-permute-start.3 = (bf16[512,768]{1,0:T(8,128)(2,1)S(1)}, bf16[512,768]{1,0:T(8,128)(2,1)S(1)}, u32[]{:S(2)}, u32[]{:S(2)}) collective-permute-start(bf16[512,768]{1,0:T(8,128)(2,1)S(1)} %bitcast.6), channel_id=1, source_target_pairs={{0,6},{1,7},{2,4},{3,5},{4,10},{5,11},{6,8},{7,9},{8,14},{9,15},{1... | collective-permute-start | bytes 2359304 | tf_op jit(solution)/shard_map/ppermute | solution.py:20
  41.4 18.0 %collective-permute-start.1 = (bf16[512,768]{1,0:T(8,128)(2,1)S(1)}, bf16[512,768]{1,0:T(8,128)(2,1)S(1)}, u32[]{:S(2)}, u32[]{:S(2)}) collective-permute-start(bf16[512,768]{1,0:T(8,128)(2,1)S(1)} %bitcast.7), channel_id=1, source_target_pairs={{0,2},{1,3},{2,0},{3,1},{4,6},{5,7},{6,4},{7,5},{8,10},{9,11},{10,... | collective-permute-start | bytes 2359304 | tf_op jit(solution)/shard_map/ppermute | solution.py:20
  41.4 21.3 %collective-permute-start = (bf16[512,768]{1,0:T(8,128)(2,1)S(1)}, bf16[512,768]{1,0:T(8,128)(2,1)S(1)}, u32[]{:S(2)}, u32[]{:S(2)}) collective-permute-start(bf16[512,768]{1,0:T(8,128)(2,1)S(1)} %bitcast.8), channel_id=1, source_target_pairs={{0,248},{1,249},{2,250},{3,251},{4,252},{5,253},{6,254},{7,255},{8... | collective-permute-start | bytes 2359304 | tf_op jit(solution)/shard_map/ppermute | solution.py:20
  59.4 20.4 %collective-permute-start.2 = (bf16[512,768]{1,0:T(8,128)(2,1)S(1)}, bf16[512,768]{1,0:T(8,128)(2,1)S(1)}, u32[]{:S(2)}, u32[]{:S(2)}) collective-permute-start(bf16[512,768]{1,0:T(8,128)(2,1)S(1)} %collective-permute-done.1.refs_2_.refs_6_.refs_0_.own), channel_id=1, source_target_pairs={{0,248},{1,249},{2,250},{3,251},{4,252},{5,253},{6,254},{7,255},{8... | collective-permute-start | bytes 2359304 | tf_op jit(solution)/shard_map/ppermute | solution.py:20
  59.4 20.4 %collective-permute-start.4 = (bf16[512,768]{1,0:T(8,128)(2,1)S(1)}, bf16[512,768]{1,0:T(8,128)(2,1)S(1)}, u32[]{:S(2)}, u32[]{:S(2)}) collective-permute-start(bf16[512,768]{1,0:T(8,128)(2,1)S(1)} %collective-permute-done.3.refs_2_.refs_0_), channel_id=1, source_target_pairs={{0,2},{1,3},{2,0},{3,1},{4,6},{5,7},{6,4},{7,5},{8,10},{9,11},{10,... | collective-permute-start | bytes 2359304 | tf_op jit(solution)/shard_map/ppermute | solution.py:20
  59.7 20.6 %collective-permute-start.5 = (bf16[512,768]{1,0:T(8,128)(2,1)S(1)}, bf16[512,768]{1,0:T(8,128)(2,1)S(1)}, u32[]{:S(2)}, u32[]{:S(2)}) collective-permute-start(bf16[512,768]{1,0:T(8,128)(2,1)S(1)} %collective-permute-done.1.refs_2_.refs_6_.refs_0_.own), channel_id=1, source_target_pairs={{0,1},{1,0},{2,3},{3,2},{4,5},{5,4},{6,7},{7,6},{8,9},{9,8},{10,11... | collective-permute-start | bytes 2359304 | tf_op jit(solution)/shard_map/ppermute | solution.py:20
  59.7 20.7 %collective-permute-start.13 = (bf16[512,768]{1,0:T(8,128)(2,1)S(1)}, bf16[512,768]{1,0:T(8,128)(2,1)S(1)}, u32[]{:S(2)}, u32[]{:S(2)}) collective-permute-start(bf16[512,768]{1,0:T(8,128)(2,1)S(1)} %collective-permute-done.3.refs_2_.refs_0_), channel_id=1, source_target_pairs={{0,1},{1,0},{2,3},{3,2},{4,5},{5,4},{6,7},{7,6},{8,9},{9,8},{10,11... | collective-permute-start | bytes 2359304 | tf_op jit(solution)/shard_map/ppermute | solution.py:20
  62.7 28.5 %collective-permute-start.11 = (bf16[768,768]{1,0:T(8,128)(2,1)S(1)}, bf16[768,768]{1,0:T(8,128)(2,1)S(1)}, u32[]{:S(2)}, u32[]{:S(2)}) collective-permute-start(bf16[768,768]{1,0:T(8,128)(2,1)S(1)} %away.1), channel_id=1, source_target_pairs={{0,6},{1,7},{2,4},{3,5},{4,10},{5,11},{6,8},{7,9},{8,14},{9,15},{1... | collective-permute-start | bytes 3538952 | tf_op jit(solution)/shard_map/ppermute | solution.py:20
  79.7 2.4 %collective-permute-start.6 = (bf16[512,768]{1,0:T(8,128)(2,1)S(1)}, bf16[512,768]{1,0:T(8,128)(2,1)S(1)}, u32[]{:S(2)}, u32[]{:S(2)}) collective-permute-start(bf16[512,768]{1,0:T(8,128)(2,1)S(1)} %bitcast.9), channel_id=1, source_target_pairs={{0,1},{1,0},{2,3},{3,2},{4,5},{5,4},{6,7},{7,6},{8,9},{9,8},{10,11... | collective-permute-start | bytes 2359304 | tf_op jit(solution)/shard_map/ppermute | solution.py:20
  79.7 3.4 %collective-permute-start.9 = (bf16[512,768]{1,0:T(8,128)(2,1)S(1)}, bf16[512,768]{1,0:T(8,128)(2,1)S(1)}, u32[]{:S(2)}, u32[]{:S(2)}) collective-permute-start(bf16[512,768]{1,0:T(8,128)(2,1)S(1)} %collective-permute-done.refs_2_.refs_4_.ahead), channel_id=1, source_target_pairs={{0,1},{1,0},{2,3},{3,2},{4,5},{5,4},{6,7},{7,6},{8,9},{9,8},{10,11... | collective-permute-start | bytes 2359304 | tf_op jit(solution)/shard_map/ppermute | solution.py:20
  80.2 4.3 %collective-permute-start.8 = (bf16[512,768]{1,0:T(8,128)(2,1)S(1)}, bf16[512,768]{1,0:T(8,128)(2,1)S(1)}, u32[]{:S(2)}, u32[]{:S(2)}) collective-permute-start(bf16[512,768]{1,0:T(8,128)(2,1)S(1)} %collective-permute-done.2.refs_2_.refs_6_.ahead), channel_id=1, source_target_pairs={{0,1},{1,0},{2,3},{3,2},{4,5},{5,4},{6,7},{7,6},{8,9},{9,8},{10,11... | collective-permute-start | bytes 2359304 | tf_op jit(solution)/shard_map/ppermute | solution.py:20
  80.3 6.0 %collective-permute-start.12 = (bf16[512,768]{1,0:T(8,128)(2,1)S(1)}, bf16[512,768]{1,0:T(8,128)(2,1)S(1)}, u32[]{:S(2)}, u32[]{:S(2)}) collective-permute-start(bf16[512,768]{1,0:T(8,128)(2,1)S(1)} %collective-permute-done.4.refs_0_.prev), channel_id=1, source_target_pairs={{0,1},{1,0},{2,3},{3,2},{4,5},{5,4},{6,7},{7,6},{8,9},{9,8},{10,11... | collective-permute-start | bytes 2359304 | tf_op jit(solution)/shard_map/ppermute | solution.py:20
  85.9 7.2 %collective-permute-start.10 = (bf16[384,768]{1,0:T(8,128)(2,1)S(1)}, bf16[384,768]{1,0:T(8,128)(2,1)S(1)}, u32[]{:S(2)}, u32[]{:S(2)}) collective-permute-start(bf16[384,768]{1,0:T(8,128)(2,1)S(1)} %gram.8.oa), channel_id=1, source_target_pairs={{0,1},{1,0},{2,3},{3,2},{4,5},{5,4},{6,7},{7,6},{8,9},{9,8},{10,11... | collective-permute-start | bytes 1769480 | tf_op jit(solution)/shard_map/ppermute | solution.py:20
  91.8 2.1 %collective-permute-start.15 = (bf16[384,768]{1,0:T(8,128)(2,1)S(1)}, bf16[384,768]{1,0:T(8,128)(2,1)S(1)}, u32[]{:S(2)}, u32[]{:S(2)}) collective-permute-start(bf16[384,768]{1,0:T(8,128)(2,1)S(1)} %screen.3.pa), channel_id=1, source_target_pairs={{0,1},{1,0},{2,3},{3,2},{4,5},{5,4},{6,7},{7,6},{8,9},{9,8},{10,11... | collective-permute-start | bytes 1769480 | tf_op jit(solution)/shard_map/ppermute | solution.py:20
  92.6 7.2 %collective-permute-start.14 = (bf16[384,768]{1,0:T(8,128)(2,1)S(1)}, bf16[384,768]{1,0:T(8,128)(2,1)S(1)}, u32[]{:S(2)}, u32[]{:S(2)}) collective-permute-start(bf16[384,768]{1,0:T(8,128)(2,1)S(1)} %screen.2.po), channel_id=1, source_target_pairs={{0,1},{1,0},{2,3},{3,2},{4,5},{5,4},{6,7},{7,6},{8,9},{9,8},{10,11... | collective-permute-start | bytes 1769480 | tf_op jit(solution)/shard_map/ppermute | solution.py:20
  96.3 20.6 %collective-permute-start.17 = (bf16[512,768]{1,0:T(8,128)(2,1)S(1)}, bf16[512,768]{1,0:T(8,128)(2,1)S(1)}, u32[]{:S(2)}, u32[]{:S(2)}) collective-permute-start(bf16[512,768]{1,0:T(8,128)(2,1)S(1)} %to_ahead_kernel.1), channel_id=1, source_target_pairs={{0,8},{1,9},{2,10},{3,11},{4,12},{5,13},{6,14},{7,15},{8,16},{9,17... | collective-permute-start | bytes 2359304 | tf_op jit(solution)/shard_map/ppermute | solution.py:20
  102.1 24.8 %collective-permute-start.16 = (bf16[512,768]{1,0:T(8,128)(2,1)S(1)}, bf16[512,768]{1,0:T(8,128)(2,1)S(1)}, u32[]{:S(2)}, u32[]{:S(2)}) collective-permute-start(bf16[512,768]{1,0:T(8,128)(2,1)S(1)} %to_prev_kernel.1), channel_id=1, source_target_pairs={{0,254},{1,255},{2,252},{3,253},{4,2},{5,3},{6,0},{7,1},{8,6},{9,7... | collective-permute-start | bytes 2359304 | tf_op jit(solution)/shard_map/ppermute | solution.py:20
  109.3 2.1 %collective-permute-start.7 = (bf16[384,768]{1,0:T(8,128)(2,1)S(1)}, bf16[384,768]{1,0:T(8,128)(2,1)S(1)}, u32[]{:S(2)}, u32[]{:S(2)}) collective-permute-start(bf16[384,768]{1,0:T(8,128)(2,1)S(1)} %gram.6.oo), channel_id=1, source_target_pairs={{0,1},{1,0},{2,3},{3,2},{4,5},{5,4},{6,7},{7,6},{8,9},{9,8},{10,11... | collective-permute-start | bytes 1769480 | tf_op jit(solution)/shard_map/ppermute | solution.py:20

commit v5 on v4

--- a/solution.py
+++ b/solution.py
@@ -172,7 +172,7 @@
     )
 
 
-def group_kernel(scalars, order, orbitals, out):
+def group_kernel(order, orbitals, out):
     bricks = out.shape[2] // TILE
     for region in range(out.shape[0]):
         for brick in range(bricks):
@@ -180,21 +180,21 @@
             out[region, :, brick * TILE : (brick + 1) * TILE] = orbitals[:, pl.ds(start, TILE)]
 
 
-def grouped_by_region(scalars, order, orbitals, points):
+def grouped_by_region(order, orbitals, points):
     shape = (orbitals.shape[1] // points, orbitals.shape[0], points)
     return pl.pallas_call(
         group_kernel,
         grid_spec=pltpu.PrefetchScalarGridSpec(
-            num_scalar_prefetch=2,
+            num_scalar_prefetch=1,
             grid=(1,),
-            in_specs=[pl.BlockSpec(orbitals.shape, lambda i, s, o: (0, 0))],
-            out_specs=pl.BlockSpec(shape, lambda i, s, o: (0, 0, 0)),
+            in_specs=[pl.BlockSpec(orbitals.shape, lambda i, o: (0, 0))],
+            out_specs=pl.BlockSpec(shape, lambda i, o: (0, 0, 0)),
         ),
         out_shape=jax.ShapeDtypeStruct(shape, orbitals.dtype),
         compiler_params=pltpu.CompilerParams(vmem_limit_bytes=24 * 2**20),
         cost_estimate=pl.CostEstimate(flops=0, bytes_accessed=0, transcendentals=0),
         name="group",
-    )(scalars, order, orbitals)
+    )(order, orbitals)
 
 
 def per_device(orbitals, point_region, coulomb, pair_mask):
@@ -209,7 +209,7 @@
     )
     rank = jnp.sum(before.astype(jnp.int32), axis=1)
     order = jnp.sum(jnp.where(rank[:, None] == region[None, :], region[:, None], 0), axis=0)
-    grouped = grouped_by_region(scalars, order, orbitals, coulomb.shape[2])
+    grouped = grouped_by_region(order, orbitals, coulomb.shape[2])
     own = lax.all_to_all(grouped, "region", split_axis=0, concat_axis=0, tiled=True)
     own = own.reshape(-1, coulomb.shape[2])
 

time: 130 us -> 129 us (level)
  waiting for transfers between devices: 50 us -> 47.5 us
  Pallas kernels: 21.6 us -> 23.9 us
    ppermute x18, waiting for transfers between devices: 50 us -> 47.5 us  [moved(): return lax.ppermute(array, ('region', 'orb'), pairs)]
    pallas_call x12, Pallas kernels: 20.5 us -> 22.8 us  [call(): pl.pallas_call(kernel, grid_spec=pltpu.PrefetchScalarGridSpec(num_scalar_...]
  transfers between devices with their start and end apart: 18 -> 18, of which waited for: 10 -> 9; matrix products, arithmetic and copies ran while one was open for 0% -> 0% of each run, Pallas kernels for 16% -> 18%
where the time goes in v5:
time: 129 us; the launch traced here: 127 us
  waiting for transfers between devices  47.5 us (37%)
  blocking collectives  33.1 us (26%)
  Pallas kernels  23.9 us (19%)
  starting transfers between devices  18.7 us (14%)
  local copies, waits for them, and re-layouts  2.21 us (2%)
  other arithmetic  1.87 us (1%)
    ppermute x18, waiting for transfers between devices, moved(): return lax.ppermute(array, ('region', 'orb'), pairs)  47.5 us
    all_to_all x1, blocking collectives, per_device(): lax.all_to_all(grouped, 'region', split_axis=0, concat_axis=0, tiled=True)  33.1 us
    pallas_call x12, Pallas kernels, call(): pl.pallas_call(kernel, grid_spec=pltpu.PrefetchScalarGridSpec(num_scalar_...  22.8 us
    ppermute x18, starting transfers between devices, moved(): return lax.ppermute(array, ('region', 'orb'), pairs)  18.7 us
  transfers between devices with their start and end apart: 18, of which 9 were waited for; matrix products, arithmetic and copies ran while one was open for 0% of the time, Pallas kernels for 18%

profile of v5, /device:TPU:126, one launch (start us, length us, event | category | flops | bytes accessed | tf_op | source)
XLA Modules:
  0.0 127.4 jit_solution(10871812910331361425)
XLA Ops:
  0.0 1.1 slice_reduce_fusion
  1.5 1.1 copy-done
  2.6 1.1 group.1
  3.7 33.1 %all_to_all.5 = bf16[64,8,768]{2,1,0:T(8,128)(2,1)S(1)} all-to-all(bf16[64,8,768]{2,1,0:T(8,128)(2,1)S(1)} %group.1), channel_id=1, replica_groups=mesh['region'=64,'orb'=4] {'region'}, dimensions={0} | all-to-all | bytes 1572864 | tf_op jit(solution)/shard_map/all_to_all | solution.py:213
  36.8 3.8 %collective-permute-start.3 = (bf16[512,768]{1,0:T(8,128)(2,1)S(1)}, bf16[512,768]{1,0:T(8,128)(2,1)}, u32[]{:S(2)}, u32[]{:S(2)}) collective-permute-start(bf16[512,768]{1,0:T(8,128)(2,1)S(1)} %bitcast.6), channel_id=1, source_target_pairs={{0,6},{1,7},{2,4},{3,5},{4,10},{5,11},{6,8},{7,9},{8,14},{9,15},{1... | collective-permute-start | bytes 2359304 | tf_op jit(solution)/shard_map/ppermute | solution.py:20
  40.8 2.1 %away.1 = bf16[768,768]{1,0:T(8,128)(2,1)S(1)} custom-call(s32[4]{0:T(128)S(1)} %pad_add_fusion.scalars, bf16[1,4,768,768]{3,2,1,0:T(8,128)(2,1)} %refs_5_.1, bf16[1,4,768,768]{3,2,1,0:T(8,128)(2,1)} %refs_5_.1), custom_call_target="tpu_custom_call" | custom-call | tf_op jit(solution)/shard_map/away/pallas_call | solution.py:24
  43.0 13.3 %collective-permute-done.3.refs_2_.refs_0_ = bf16[512,768]{1,0:T(8,128)(2,1)} collective-permute-done((bf16[512,768]{1,0:T(8,128)(2,1)S(1)}, bf16[512,768]{1,0:T(8,128)(2,1)}, u32[]{:S(2)}, u32[]{:S(2)}) %collective-permute-start.3) | collective-permute-done | bytes 786464 | tf_op jit(solution)/shard_map/ppermute | solution.py:20
  56.3 2.2 %collective-permute-done.1.refs_2_.refs_6_.refs_0_.own = bf16[512,768]{1,0:T(8,128)(2,1)S(1)} collective-permute-done((bf16[512,768]{1,0:T(8,128)(2,1)S(1)}, bf16[512,768]{1,0:T(8,128)(2,1)S(1)}, u32[]{:S(2)}, u32[]{:S(2)}) %collective-permute-start.1) | collective-permute-done | bytes 786464 | tf_op jit(solution)/shard_map/ppermute | solution.py:20
  58.8 0.5 collective-permute-start.13
  59.3 2.5 %collective-permute-done.refs_2_.refs_4_.ahead = bf16[512,768]{1,0:T(8,128)(2,1)S(1)} collective-permute-done((bf16[512,768]{1,0:T(8,128)(2,1)S(1)}, bf16[512,768]{1,0:T(8,128)(2,1)S(1)}, u32[]{:S(2)}, u32[]{:S(2)}) %collective-permute-start) | collective-permute-done | bytes 786464 | tf_op jit(solution)/shard_map/ppermute | solution.py:20
  61.8 3.1 %collective-permute-start.11 = (bf16[768,768]{1,0:T(8,128)(2,1)S(1)}, bf16[768,768]{1,0:T(8,128)(2,1)S(1)}, u32[]{:S(2)}, u32[]{:S(2)}) collective-permute-start(bf16[768,768]{1,0:T(8,128)(2,1)S(1)} %away.1), channel_id=1, source_target_pairs={{0,6},{1,7},{2,4},{3,5},{4,10},{5,11},{6,8},{7,9},{8,14},{9,15},{1... | collective-permute-start | bytes 3538952 | tf_op jit(solution)/shard_map/ppermute | solution.py:20
  64.9 13.9 %collective-permute-done.2.refs_2_.refs_6_.ahead = bf16[512,768]{1,0:T(8,128)(2,1)S(1)} collective-permute-done((bf16[512,768]{1,0:T(8,128)(2,1)S(1)}, bf16[512,768]{1,0:T(8,128)(2,1)S(1)}, u32[]{:S(2)}, u32[]{:S(2)}) %collective-permute-start.2) | collective-permute-done | bytes 786464 | tf_op jit(solution)/shard_map/ppermute | solution.py:20
  78.9 0.5 collective-permute-start.9
  79.9 2.3 %gram.10.refs_4_ = f32[384,768]{1,0:T(8,128)S(1)} custom-call(s32[4]{0:T(128)S(1)} %pad_add_fusion.scalars, bf16[512,768]{1,0:T(8,128)(2,1)} %collective-permute-done.3.refs_2_.refs_0_, bf16[512,768]{1,0:T(8,128)(2,1)S(1)} %collective-permute-done.13.refs_3_.refs_1_, bf16[512,768]{1,0:T(8,128)(2,1)S(1)} %collective-permute-done.1.refs_2_.refs_6_.refs_0_.own, ...), custom_call_target="tpu_custom_call" | custom-call | tf_op jit(solution)/shard_map/gram/pallas_call | solution.py:24
  82.3 1.4 %gram.7.refs_4_ = f32[384,768]{1,0:T(8,128)S(1)} custom-call(s32[4]{0:T(128)S(1)} %pad_add_fusion.scalars, bf16[512,768]{1,0:T(8,128)(2,1)S(1)} %bitcast.10, bf16[512,768]{1,0:T(8,128)(2,1)S(1)} %collective-permute-done.6.refs_1_.refs_5_.refs_3_, bf16[512,768]{1,0:T(8,128)(2,1)S(1)} %collective-permute-done.refs_2_.refs_4_.ahead, ...), custom_call_target="tpu_custom_call" | custom-call | tf_op jit(solution)/shard_map/gram/pallas_call | solution.py:24
  83.7 1.4 %gram.8.oa = bf16[384,768]{1,0:T(8,128)(2,1)S(1)} custom-call(s32[4]{0:T(128)S(1)} %pad_add_fusion.scalars, bf16[512,768]{1,0:T(8,128)(2,1)S(1)} %collective-permute-done.1.refs_2_.refs_6_.refs_0_.own, bf16[512,768]{1,0:T(8,128)(2,1)S(1)} %collective-permute-done.5.refs_3_.refs_7_.refs_1_, bf16[512,768]{1,0:T(8,128)(2,1)S(1)} %collective-permute-done.2.refs_2_.refs_6_.ahead, ...), custom_call_target="tpu_custom_call" | custom-call | tf_op jit(solution)/shard_map/gram/pallas_call | solution.py:24
  85.5 3.1 %gram.9 = f32[384,768]{1,0:T(8,128)S(1)} custom-call(s32[4]{0:T(128)S(1)} %pad_add_fusion.scalars, bf16[512,768]{1,0:T(8,128)(2,1)S(1)} %collective-permute-done.4.refs_0_.prev, bf16[512,768]{1,0:T(8,128)(2,1)S(1)} %collective-permute-done.12.refs_1_, bf16[512,768]{1,0:T(8,128)(2,1)} %collective-permute-done.3.refs_2_.refs_0_, ...), custom_call_target="tpu_custom_call" | custom-call | tf_op jit(solution)/shard_map/gram/pallas_call | solution.py:24
  88.6 1.4 %gram.11 = f32[384,768]{1,0:T(8,128)S(1)} custom-call(s32[4]{0:T(128)S(1)} %pad_add_fusion.scalars, bf16[512,768]{1,0:T(8,128)(2,1)S(1)} %collective-permute-done.4.refs_0_.prev, bf16[512,768]{1,0:T(8,128)(2,1)S(1)} %collective-permute-done.12.refs_1_, bf16[512,768]{1,0:T(8,128)(2,1)S(1)} %bitcast.11, ...), custom_call_target="tpu_custom_call" | custom-call | tf_op jit(solution)/shard_map/gram/pallas_call | solution.py:24
  90.4 0.6 screen.3.pa
  91.2 0.6 screen.2.po
  91.8 0.6 collective-permute-start.14
  92.4 0.8 collective-permute-done.15.pa_too
  93.2 2.3 %to_ahead_kernel.1 = bf16[512,768]{1,0:T(8,128)(2,1)S(1)} custom-call(s32[4]{0:T(128)S(1)} %pad_add_fusion.scalars, bf16[512,768]{1,0:T(8,128)(2,1)S(1)} %bitcast.12, bf16[512,768]{1,0:T(8,128)(2,1)S(1)} %collective-permute-done.4.refs_0_.prev, bf16[384,768]{1,0:T(8,128)(2,1)S(1)} %gram.8.oa, bf16[384,768]{1,0:T(8,128)(2,1)S(1)} %collective-permute-done.10.oa_too, ...), custom_call_target="tpu_custom_call" | custom-call | tf_op jit(solution)/shard_map/to_ahead_kernel/pallas_call | solution.py:24
  95.5 3.4 %collective-permute-start.17 = (bf16[512,768]{1,0:T(8,128)(2,1)S(1)}, bf16[512,768]{1,0:T(8,128)(2,1)S(1)}, u32[]{:S(2)}, u32[]{:S(2)}) collective-permute-start(bf16[512,768]{1,0:T(8,128)(2,1)S(1)} %to_ahead_kernel.1), channel_id=1, source_target_pairs={{0,8},{1,9},{2,10},{3,11},{4,12},{5,13},{6,14},{7,15},{8,16},{9,17... | collective-permute-start | bytes 2359304 | tf_op jit(solution)/shard_map/ppermute | solution.py:20
  98.9 2.3 %to_prev_kernel.1 = bf16[512,768]{1,0:T(8,128)(2,1)S(1)} custom-call(s32[4]{0:T(128)S(1)} %pad_add_fusion.scalars, bf16[512,768]{1,0:T(8,128)(2,1)S(1)} %collective-permute-done.1.refs_2_.refs_6_.refs_0_.own, bf16[512,768]{1,0:T(8,128)(2,1)S(1)} %collective-permute-done.2.refs_2_.refs_6_.ahead, bf16[384,768]{1,0:T(8,128)(2,1)S(1)} %screen.2.po, ...), custom_call_target="tpu_custom_call" | custom-call | tf_op jit(solution)/shard_map/to_prev_kernel/pallas_call | solution.py:24
  101.2 5.2 %collective-permute-start.16 = (bf16[512,768]{1,0:T(8,128)(2,1)S(1)}, bf16[512,768]{1,0:T(8,128)(2,1)S(1)}, u32[]{:S(2)}, u32[]{:S(2)}) collective-permute-start(bf16[512,768]{1,0:T(8,128)(2,1)S(1)} %to_prev_kernel.1), channel_id=1, source_target_pairs={{0,254},{1,255},{2,252},{3,253},{4,2},{5,3},{6,0},{7,1},{8,6},{9,7... | collective-permute-start | bytes 2359304 | tf_op jit(solution)/shard_map/ppermute | solution.py:20
  106.5 2.0 %gram.6.oo = bf16[384,768]{1,0:T(8,128)(2,1)S(1)} custom-call(s32[4]{0:T(128)S(1)} %pad_add_fusion.scalars, bf16[512,768]{1,0:T(8,128)(2,1)S(1)} %bitcast.13, bf16[512,768]{1,0:T(8,128)(2,1)S(1)} %collective-permute-done.6.refs_1_.refs_5_.refs_3_, bf16[512,768]{1,0:T(8,128)(2,1)S(1)} %collective-permute-done.1.refs_2_.refs_6_.refs_0_.own, ...), custom_call_target="tpu_custom_call" | custom-call | tf_op jit(solution)/shard_map/gram/pallas_call | solution.py:24
  108.6 2.0 %collective-permute-done.7.oo_too = bf16[384,768]{1,0:T(8,128)(2,1)S(1)} collective-permute-done((bf16[384,768]{1,0:T(8,128)(2,1)S(1)}, bf16[384,768]{1,0:T(8,128)(2,1)S(1)}, u32[]{:S(2)}, u32[]{:S(2)}) %collective-permute-start.7) | collective-permute-done | bytes 589856 | tf_op jit(solution)/shard_map/ppermute | solution.py:20
  110.6 3.2 %stay_kernel.1 = f32[512,768]{1,0:T(8,128)S(1)} custom-call(s32[4]{0:T(128)S(1)} %pad_add_fusion.scalars, bf16[512,768]{1,0:T(8,128)(2,1)S(1)} %bitcast.15, bf16[512,768]{1,0:T(8,128)(2,1)S(1)} %collective-permute-done.refs_2_.refs_4_.ahead, bf16[512,768]{1,0:T(8,128)(2,1)S(1)} %collective-permute-done.4.refs_0_.prev, bf16[384,768]{1,0:T(8,128)(2,1)S(1)} %gram.6.oo, ...), custom_call_target="tpu_custom_call" | custom-call | tf_op jit(solution)/shard_map/stay_kernel/pallas_call | solution.py:24
  113.7 2.2 %collective-permute-done.17 = bf16[512,768]{1,0:T(8,128)(2,1)S(1)} collective-permute-done((bf16[512,768]{1,0:T(8,128)(2,1)S(1)}, bf16[512,768]{1,0:T(8,128)(2,1)S(1)}, u32[]{:S(2)}, u32[]{:S(2)}) %collective-permute-start.17) | collective-permute-done | bytes 786464 | tf_op jit(solution)/shard_map/ppermute | solution.py:20
  116.0 10.0 %collective-permute-done.16 = bf16[512,768]{1,0:T(8,128)(2,1)S(1)} collective-permute-done((bf16[512,768]{1,0:T(8,128)(2,1)S(1)}, bf16[512,768]{1,0:T(8,128)(2,1)S(1)}, u32[]{:S(2)}, u32[]{:S(2)}) %collective-permute-start.16) | collective-permute-done | bytes 786464 | tf_op jit(solution)/shard_map/ppermute | solution.py:20
  126.0 1.4 %add_multiply_fusion = f32[512,768]{1,0:T(8,128)} fusion(bf16[512,768]{1,0:T(8,128)(2,1)S(1)} %collective-permute-done.17, f32[512,768]{1,0:T(8,128)S(1)} %stay_kernel.1, bf16[512,768]{1,0:T(8,128)(2,1)S(1)} %collective-permute-done.16), kind=kLoop, calls=%fused_computation | loop fusion | flops 1966080 | bytes 4718592 | tf_op jit(solution)/shard_map/mul | solution.py:252
  (32 shorter events, 2.6 us)
Async XLA Ops:
  1.5 1.1 copy-start
  2.6 38.1 %copy-start.1 = (s32[1,3]{1,0:T(1,128)S(1)}, s32[1,3]{1,0:T(1,128)}, u32[]{:S(2)}) copy-start(s32[1,3]{1,0:T(1,128)} %param.7) | copy-start | bytes 40
  3.7 80.0 %slice-start = ((s8[4718592]{0:T(1024)(128)(4,1)}), s8[524288]{0:T(1024)(128)(4,1)S(1)}, s32[]{:S(2)}) async-start(s8[4718592]{0:T(1024)(128)(4,1)} %bitcast.4), calls=%async_computation.1 | async-start | bytes 1048576
  36.8 19.5 %collective-permute-start.3 = (bf16[512,768]{1,0:T(8,128)(2,1)S(1)}, bf16[512,768]{1,0:T(8,128)(2,1)}, u32[]{:S(2)}, u32[]{:S(2)}) collective-permute-start(bf16[512,768]{1,0:T(8,128)(2,1)S(1)} %bitcast.6), channel_id=1, source_target_pairs={{0,6},{1,7},{2,4},{3,5},{4,10},{5,11},{6,8},{7,9},{8,14},{9,15},{1... | collective-permute-start | bytes 2359304 | tf_op jit(solution)/shard_map/ppermute | solution.py:20
  40.5 18.0 %collective-permute-start.1 = (bf16[512,768]{1,0:T(8,128)(2,1)S(1)}, bf16[512,768]{1,0:T(8,128)(2,1)S(1)}, u32[]{:S(2)}, u32[]{:S(2)}) collective-permute-start(bf16[512,768]{1,0:T(8,128)(2,1)S(1)} %bitcast.7), channel_id=1, source_target_pairs={{0,2},{1,3},{2,0},{3,1},{4,6},{5,7},{6,4},{7,5},{8,10},{9,11},{10,... | collective-permute-start | bytes 2359304 | tf_op jit(solution)/shard_map/ppermute | solution.py:20
  40.5 21.3 %collective-permute-start = (bf16[512,768]{1,0:T(8,128)(2,1)S(1)}, bf16[512,768]{1,0:T(8,128)(2,1)S(1)}, u32[]{:S(2)}, u32[]{:S(2)}) collective-permute-start(bf16[512,768]{1,0:T(8,128)(2,1)S(1)} %bitcast.8), channel_id=1, source_target_pairs={{0,248},{1,249},{2,250},{3,251},{4,252},{5,253},{6,254},{7,255},{8... | collective-permute-start | bytes 2359304 | tf_op jit(solution)/shard_map/ppermute | solution.py:20
  40.8 42.9 %slice-start.1 = ((s8[4718592]{0:T(1024)(128)(4,1)}), s8[4194304]{0:T(1024)(128)(4,1)S(1)}, s32[]{:S(2)}) async-start(s8[4718592]{0:T(1024)(128)(4,1)} %bitcast.4), calls=%async_computation.2 | async-start | bytes 8388608
  58.5 20.4 %collective-permute-start.2 = (bf16[512,768]{1,0:T(8,128)(2,1)S(1)}, bf16[512,768]{1,0:T(8,128)(2,1)S(1)}, u32[]{:S(2)}, u32[]{:S(2)}) collective-permute-start(bf16[512,768]{1,0:T(8,128)(2,1)S(1)} %collective-permute-done.1.refs_2_.refs_6_.refs_0_.own), channel_id=1, source_target_pairs={{0,248},{1,249},{2,250},{3,251},{4,252},{5,253},{6,254},{7,255},{8... | collective-permute-start | bytes 2359304 | tf_op jit(solution)/shard_map/ppermute | solution.py:20
  58.5 20.4 %collective-permute-start.4 = (bf16[512,768]{1,0:T(8,128)(2,1)}, bf16[512,768]{1,0:T(8,128)(2,1)S(1)}, u32[]{:S(2)}, u32[]{:S(2)}) collective-permute-start(bf16[512,768]{1,0:T(8,128)(2,1)} %collective-permute-done.3.refs_2_.refs_0_), channel_id=1, source_target_pairs={{0,2},{1,3},{2,0},{3,1},{4,6},{5,7},{6,4},{7,5},{8,10},{9,11},{10,... | collective-permute-start | bytes 2359304 | tf_op jit(solution)/shard_map/ppermute | solution.py:20
  58.8 20.6 %collective-permute-start.5 = (bf16[512,768]{1,0:T(8,128)(2,1)S(1)}, bf16[512,768]{1,0:T(8,128)(2,1)S(1)}, u32[]{:S(2)}, u32[]{:S(2)}) collective-permute-start(bf16[512,768]{1,0:T(8,128)(2,1)S(1)} %collective-permute-done.1.refs_2_.refs_6_.refs_0_.own), channel_id=1, source_target_pairs={{0,1},{1,0},{2,3},{3,2},{4,5},{5,4},{6,7},{7,6},{8,9},{9,8},{10,11... | collective-permute-start | bytes 2359304 | tf_op jit(solution)/shard_map/ppermute | solution.py:20
  58.8 20.7 %collective-permute-start.13 = (bf16[512,768]{1,0:T(8,128)(2,1)}, bf16[512,768]{1,0:T(8,128)(2,1)S(1)}, u32[]{:S(2)}, u32[]{:S(2)}) collective-permute-start(bf16[512,768]{1,0:T(8,128)(2,1)} %collective-permute-done.3.refs_2_.refs_0_), channel_id=1, source_target_pairs={{0,1},{1,0},{2,3},{3,2},{4,5},{5,4},{6,7},{7,6},{8,9},{9,8},{10,11... | collective-permute-start | bytes 2359304 | tf_op jit(solution)/shard_map/ppermute | solution.py:20
  61.8 28.6 %collective-permute-start.11 = (bf16[768,768]{1,0:T(8,128)(2,1)S(1)}, bf16[768,768]{1,0:T(8,128)(2,1)S(1)}, u32[]{:S(2)}, u32[]{:S(2)}) collective-permute-start(bf16[768,768]{1,0:T(8,128)(2,1)S(1)} %away.1), channel_id=1, source_target_pairs={{0,6},{1,7},{2,4},{3,5},{4,10},{5,11},{6,8},{7,9},{8,14},{9,15},{1... | collective-permute-start | bytes 3538952 | tf_op jit(solution)/shard_map/ppermute | solution.py:20
  78.9 3.4 %collective-permute-start.6 = (bf16[512,768]{1,0:T(8,128)(2,1)S(1)}, bf16[512,768]{1,0:T(8,128)(2,1)S(1)}, u32[]{:S(2)}, u32[]{:S(2)}) collective-permute-start(bf16[512,768]{1,0:T(8,128)(2,1)S(1)} %bitcast.9), channel_id=1, source_target_pairs={{0,1},{1,0},{2,3},{3,2},{4,5},{5,4},{6,7},{7,6},{8,9},{9,8},{10,11... | collective-permute-start | bytes 2359304 | tf_op jit(solution)/shard_map/ppermute | solution.py:20
  78.9 3.4 %collective-permute-start.9 = (bf16[512,768]{1,0:T(8,128)(2,1)S(1)}, bf16[512,768]{1,0:T(8,128)(2,1)S(1)}, u32[]{:S(2)}, u32[]{:S(2)}) collective-permute-start(bf16[512,768]{1,0:T(8,128)(2,1)S(1)} %collective-permute-done.refs_2_.refs_4_.ahead), channel_id=1, source_target_pairs={{0,1},{1,0},{2,3},{3,2},{4,5},{5,4},{6,7},{7,6},{8,9},{9,8},{10,11... | collective-permute-start | bytes 2359304 | tf_op jit(solution)/shard_map/ppermute | solution.py:20
  79.4 4.3 %collective-permute-start.8 = (bf16[512,768]{1,0:T(8,128)(2,1)S(1)}, bf16[512,768]{1,0:T(8,128)(2,1)S(1)}, u32[]{:S(2)}, u32[]{:S(2)}) collective-permute-start(bf16[512,768]{1,0:T(8,128)(2,1)S(1)} %collective-permute-done.2.refs_2_.refs_6_.ahead), channel_id=1, source_target_pairs={{0,1},{1,0},{2,3},{3,2},{4,5},{5,4},{6,7},{7,6},{8,9},{9,8},{10,11... | collective-permute-start | bytes 2359304 | tf_op jit(solution)/shard_map/ppermute | solution.py:20
  79.5 6.0 %collective-permute-start.12 = (bf16[512,768]{1,0:T(8,128)(2,1)S(1)}, bf16[512,768]{1,0:T(8,128)(2,1)S(1)}, u32[]{:S(2)}, u32[]{:S(2)}) collective-permute-start(bf16[512,768]{1,0:T(8,128)(2,1)S(1)} %collective-permute-done.4.refs_0_.prev), channel_id=1, source_target_pairs={{0,1},{1,0},{2,3},{3,2},{4,5},{5,4},{6,7},{7,6},{8,9},{9,8},{10,11... | collective-permute-start | bytes 2359304 | tf_op jit(solution)/shard_map/ppermute | solution.py:20
  85.1 7.3 %collective-permute-start.10 = (bf16[384,768]{1,0:T(8,128)(2,1)S(1)}, bf16[384,768]{1,0:T(8,128)(2,1)S(1)}, u32[]{:S(2)}, u32[]{:S(2)}) collective-permute-start(bf16[384,768]{1,0:T(8,128)(2,1)S(1)} %gram.8.oa), channel_id=1, source_target_pairs={{0,1},{1,0},{2,3},{3,2},{4,5},{5,4},{6,7},{7,6},{8,9},{9,8},{10,11... | collective-permute-start | bytes 1769480 | tf_op jit(solution)/shard_map/ppermute | solution.py:20
  91.1 2.1 %collective-permute-start.15 = (bf16[384,768]{1,0:T(8,128)(2,1)S(1)}, bf16[384,768]{1,0:T(8,128)(2,1)S(1)}, u32[]{:S(2)}, u32[]{:S(2)}) collective-permute-start(bf16[384,768]{1,0:T(8,128)(2,1)S(1)} %screen.3.pa), channel_id=1, source_target_pairs={{0,1},{1,0},{2,3},{3,2},{4,5},{5,4},{6,7},{7,6},{8,9},{9,8},{10,11... | collective-permute-start | bytes 1769480 | tf_op jit(solution)/shard_map/ppermute | solution.py:20
  91.8 7.1 %collective-permute-start.14 = (bf16[384,768]{1,0:T(8,128)(2,1)S(1)}, bf16[384,768]{1,0:T(8,128)(2,1)S(1)}, u32[]{:S(2)}, u32[]{:S(2)}) collective-permute-start(bf16[384,768]{1,0:T(8,128)(2,1)S(1)} %screen.2.po), channel_id=1, source_target_pairs={{0,1},{1,0},{2,3},{3,2},{4,5},{5,4},{6,7},{7,6},{8,9},{9,8},{10,11... | collective-permute-start | bytes 1769480 | tf_op jit(solution)/shard_map/ppermute | solution.py:20
  95.5 20.5 %collective-permute-start.17 = (bf16[512,768]{1,0:T(8,128)(2,1)S(1)}, bf16[512,768]{1,0:T(8,128)(2,1)S(1)}, u32[]{:S(2)}, u32[]{:S(2)}) collective-permute-start(bf16[512,768]{1,0:T(8,128)(2,1)S(1)} %to_ahead_kernel.1), channel_id=1, source_target_pairs={{0,8},{1,9},{2,10},{3,11},{4,12},{5,13},{6,14},{7,15},{8,16},{9,17... | collective-permute-start | bytes 2359304 | tf_op jit(solution)/shard_map/ppermute | solution.py:20
  101.2 24.8 %collective-permute-start.16 = (bf16[512,768]{1,0:T(8,128)(2,1)S(1)}, bf16[512,768]{1,0:T(8,128)(2,1)S(1)}, u32[]{:S(2)}, u32[]{:S(2)}) collective-permute-start(bf16[512,768]{1,0:T(8,128)(2,1)S(1)} %to_prev_kernel.1), channel_id=1, source_target_pairs={{0,254},{1,255},{2,252},{3,253},{4,2},{5,3},{6,0},{7,1},{8,6},{9,7... | collective-permute-start | bytes 2359304 | tf_op jit(solution)/shard_map/ppermute | solution.py:20
  108.5 2.1 %collective-permute-start.7 = (bf16[384,768]{1,0:T(8,128)(2,1)S(1)}, bf16[384,768]{1,0:T(8,128)(2,1)S(1)}, u32[]{:S(2)}, u32[]{:S(2)}) collective-permute-start(bf16[384,768]{1,0:T(8,128)(2,1)S(1)} %gram.6.oo), channel_id=1, source_target_pairs={{0,1},{1,0},{2,3},{3,2},{4,5},{5,4},{6,7},{7,6},{8,9},{9,8},{10,11... | collective-permute-start | bytes 1769480 | tf_op jit(solution)/shard_map/ppermute | solution.py:20
